TPU v7x, 512 devices: a whole 4x8x8 slice. The times are simulated.
512 devices in a mesh: rows: 8 (over x, core), cols: 64 (over y, z).
Axes of the slice: x: 4, y: 8, z: 8, core: 2. Of those that a mesh axis runs over, the one named last changes fastest.
Arguments:
- blocks: bfloat16 [8, 64, 96, 128, 128], P('rows', 'cols'), may hold values from -0.0048828125 to 0.0048828125
- block_row: int32 [8, 64, 96], P('rows', 'cols'), may hold values from 0 to 7
- block_col: int32 [8, 64, 96], P('rows', 'cols'), may hold values from 0 to 15
- counts: int32 [8, 64], P('rows', 'cols'), may hold values from 32 to 96, as said below
- start_block: bfloat16 [131072, 256], P(('cols', 'rows')), may hold values from -6 to 6
Outputs:
- basis: float32 [131072, 256], P(('cols', 'rows'))
- factor: float32 [256, 256], replicated
Inputs may be any that keep to these rules, and one draw needn't show every extreme that they name: `counts`: some tile has all 96 slots live.
All inputs are finite; a program needn't handle non-finite values.
Results may differ from a plain program's by a relative error of at most 0.0044.
Values may be sent and summed in bfloat16 or wider, within the bound.
A program may use at most 64 MiB of HBM per device.

v0:
```python
import math

import jax
import jax.numpy as jnp
from jax import lax
from jax.sharding import PartitionSpec as P

BS = 128
UT = 1024
IT = 2048


def swapped(block, axis, stride):
    count = lax.axis_size(axis)
    route = []
    for low in range(count):
        high = low | 1 << stride
        if high != low and high < count:
            route += [(low, high), (high, low)]
    return lax.ppermute(block, axis, route)


def forward_tile(tiles, rows_idx, cols_idx, active, panel):
    slots = tiles.shape[0]
    group = math.gcd(slots, 32)
    width = panel.shape[1]
    panel_blocks = panel.reshape(IT // BS, BS, width)

    def forward_step(carry, index):
        start = index * group
        tiles_g = lax.dynamic_slice_in_dim(tiles, start, group, 0)
        rows_g = lax.dynamic_slice_in_dim(rows_idx, start, group, 0)
        cols_g = lax.dynamic_slice_in_dim(cols_idx, start, group, 0)
        act_g = lax.dynamic_slice_in_dim(active, start, group, 0)
        pieces = jnp.take(panel_blocks, cols_g, axis=0)
        product = jnp.einsum("nab,nbk->nak", tiles_g, pieces, preferred_element_type=jnp.float32)
        onehot = (rows_g[:, None] == jnp.arange(UT // BS)[None, :]).astype(jnp.float32) * act_g[
            :, None
        ]
        return (
            carry + jnp.einsum("nu,nak->uak", onehot, product, precision=lax.Precision.HIGHEST),
            None,
        )

    total, _ = lax.scan(
        forward_step, jnp.zeros((UT // BS, BS, width), jnp.float32), jnp.arange(slots // group)
    )
    return total.reshape(UT, width)


def backward_tile(tiles, rows_idx, cols_idx, active, user_tile):
    slots = tiles.shape[0]
    group = math.gcd(slots, 32)
    width = user_tile.shape[1]
    user_blocks = user_tile.reshape(UT // BS, BS, width)

    def backward_step(carry, index):
        start = index * group
        tiles_g = lax.dynamic_slice_in_dim(tiles, start, group, 0)
        rows_g = lax.dynamic_slice_in_dim(rows_idx, start, group, 0)
        cols_g = lax.dynamic_slice_in_dim(cols_idx, start, group, 0)
        act_g = lax.dynamic_slice_in_dim(active, start, group, 0)
        pieces = jnp.take(user_blocks, rows_g, axis=0)
        product = jnp.einsum("nab,nak->nbk", tiles_g, pieces, preferred_element_type=jnp.float32)
        onehot = (cols_g[:, None] == jnp.arange(IT // BS)[None, :]).astype(jnp.float32) * act_g[
            :, None
        ]
        return (
            carry + jnp.einsum("ni,nbk->ibk", onehot, product, precision=lax.Precision.HIGHEST),
            None,
        )

    total, _ = lax.scan(
        backward_step, jnp.zeros((IT // BS, BS, width), jnp.float32), jnp.arange(slots // group)
    )
    return total.reshape(IT, width)


def local(blocks, block_row, block_col, counts, start_block):
    tiles = blocks[0, 0]
    rows_idx = block_row[0, 0]
    cols_idx = block_col[0, 0]
    active = (jnp.arange(tiles.shape[0]) < counts[0, 0]).astype(jnp.float32)
    panel = lax.all_gather(start_block, "rows", axis=0, tiled=True)
    partial_value = forward_tile(tiles, rows_idx, cols_idx, active, panel)
    user_tile = lax.psum(partial_value, "cols").astype(jnp.bfloat16)
    item_terms = backward_tile(tiles, rows_idx, cols_idx, active, user_tile)
    items = lax.psum_scatter(item_terms, "rows", scatter_dimension=0, tiled=True)
    gram_local = jnp.dot(items.T, items, precision=lax.Precision.HIGHEST)
    gram_rows = lax.psum(gram_local.astype(jnp.bfloat16), "rows").astype(jnp.float32)
    lower = jnp.linalg.cholesky(gram_rows)
    for level in range(lax.axis_size("cols").bit_length() - 1):
        partner = swapped(lower, "cols", level)
        mine = jnp.dot(lower, lower.T, precision=lax.Precision.HIGHEST)
        theirs = jnp.dot(partner, partner.T, precision=lax.Precision.HIGHEST)
        lower = jnp.linalg.cholesky(mine + theirs)
    basis = jax.scipy.linalg.solve_triangular(lower, items.T, lower=True).T
    return (basis, lower.T)


def solution(mesh):
    return jax.shard_map(
        local,
        mesh=mesh,
        in_specs=(
            P("rows", "cols", None, None, None),
            P("rows", "cols", None),
            P("rows", "cols", None),
            P("rows", "cols"),
            P(("cols", "rows"), None),
        ),
        out_specs=(P(("cols", "rows"), None), P()),
        check_vma=False,
    )
```

profile of v0, /device:TPU:1, one launch (start us, length us, event | category | flops | bytes accessed | tf_op | source)
XLA Modules:
  0.0 906.1 jit_solution(16558557929723673320)
XLA Ops:
  8.6 36.3 %all-gather.2.cloned.1.call-done = bf16[2048,256]{1,0:T(8,128)(2,1)} async-done(((bf16[256,256]{1,0:T(8,128)(2,1)}), bf16[2048,256]{1,0:T(8,128)(2,1)}) %all-gather.2.cloned.1.call-update) | async-done | bytes 1048592 | tf_op jit(solution)/shard_map/all_gather | solution.py:84
  44.9 44.8 %while.24 = (s32[]{:T(128)}, f32[8,128,256]{2,0,1:T(8,128)S(1)}, s32[3]{0:T(128)S(1)}, s32[96]{0:T(128)}, f32[96]{0:T(128)S(1)}, /*index=5*/bf16[96,128,128]{2,1...) while((s32[]{:T(128)}, f32[8,128,256]{2,0,1:T(8,128)S(1)}, ...), condition=%wide.region_1.2_spmd.clone, body=%wide.region_0.1_spmd.clone.sunk | while | flops 370673344 | bytes 17832996 | solution.py:45
  90.2 234.6 %all-reduce.5 = bf16[1024,256]{1,0:T(8,128)(2,1)S(1)} all-reduce(f32[1024,256]{1,0:T(8,128)S(1)} %bitcast.169), channel_id=1, replica_groups=mesh['rows'=8,'cols'=64] {'cols'}, use_global_device_ids=true, to_apply=%region_2.3 | all-reduce | flops 262144 | bytes 1572864 | tf_op jit(solution)/shard_map/psum | solution.py:86
  324.7 43.6 %while.25 = (s32[]{:T(128)}, f32[16,128,256]{2,0,1:T(8,128)}, s32[3]{0:T(128)S(1)}, s32[96]{0:T(128)S(1)}, f32[96]{0:T(128)S(1)}, /*index=5*/bf16[96,128,128]{2,...) while((s32[]{:T(128)}, f32[16,128,256]{2,0,1:T(8,128)}, ...), condition=%wide.region_4.5_spmd.clone, body=%wide.region_3.4_spmd.clone.sunk | while | flops 471861440 | bytes 19928584 | solution.py:73
  372.8 83.1 %reduce-scatter.2.cloned.1.call-done = f32[256,256]{1,0:T(8,128)} async-done(((f32[2048,256]{1,0:T(8,128)}), f32[256,256]{1,0:T(8,128)}) %reduce-scatter.2.cloned.1.call-update) | async-done | bytes 262160 | tf_op jit(solution)/shard_map/reduce_scatter | solution.py:88
  458.2 69.9 %all-reduce.4.cloned.1.call-done = bf16[256,256]{0,1:T(8,128)(2,1)} async-done(((bf16[256,256]{0,1:T(8,128)(2,1)}), bf16[256,256]{0,1:T(8,128)(2,1)}) %all-reduce.4.cloned.1.call-update) | async-done | bytes 131088 | tf_op jit(solution)/shard_map/psum | solution.py:90
  530.0 11.7 %cholesky.340 = f32[128,128]{1,0:T(8,128)S(1)} custom-call(f32[128,128]{1,0:T(8,128)S(1)} %cholesky.574), custom_call_target="Cholesky" | custom-call | tf_op jit(solution)/shard_map/jit(cholesky)/cholesky | solution.py:91
  552.1 11.7 %cholesky.357 = f32[128,128]{1,0:T(8,128)S(1)} custom-call(f32[128,128]{1,0:T(8,128)S(1)} %convolution_subtract_fusion.1), custom_call_target="Cholesky" | custom-call | tf_op jit(solution)/shard_map/jit(cholesky)/cholesky | solution.py:91
  574.2 11.7 %cholesky.374 = f32[128,128]{1,0:T(8,128)S(1)} custom-call(f32[128,128]{1,0:T(8,128)S(1)} %cholesky.577), custom_call_target="Cholesky" | custom-call | tf_op jit(solution)/shard_map/jit(cholesky)/cholesky | solution.py:96
  596.3 11.7 %cholesky.391 = f32[128,128]{1,0:T(8,128)S(1)} custom-call(f32[128,128]{1,0:T(8,128)S(1)} %slice_subtract_fusion.5), custom_call_target="Cholesky" | custom-call | tf_op jit(solution)/shard_map/jit(cholesky)/cholesky | solution.py:96
  614.5 12.2 %collective-permute-done.1 = f32[256,256]{1,0:T(8,128)S(1)} collective-permute-done((f32[256,256]{1,0:T(8,128)S(1)}, f32[256,256]{1,0:T(8,128)S(1)}, u32[]{:S(2)}, u32[]{:S(2)}) %collective-permute-start.1) | collective-permute-done | bytes 262176 | tf_op jit(solution)/shard_map/ppermute | solution.py:20
  627.3 11.7 %cholesky.408 = f32[128,128]{1,0:T(8,128)S(1)} custom-call(f32[128,128]{1,0:T(8,128)S(1)} %cholesky.580), custom_call_target="Cholesky" | custom-call | tf_op jit(solution)/shard_map/jit(cholesky)/cholesky | solution.py:96
  649.3 11.7 %cholesky.425 = f32[128,128]{1,0:T(8,128)S(1)} custom-call(f32[128,128]{1,0:T(8,128)S(1)} %slice_subtract_fusion.4), custom_call_target="Cholesky" | custom-call | tf_op jit(solution)/shard_map/jit(cholesky)/cholesky | solution.py:96
  670.1 12.6 %collective-permute-done.2 = f32[256,256]{1,0:T(8,128)S(1)} collective-permute-done((f32[256,256]{1,0:T(8,128)S(1)}, f32[256,256]{1,0:T(8,128)S(1)}, u32[]{:S(2)}, u32[]{:S(2)}) %collective-permute-start.2) | collective-permute-done | bytes 262176 | tf_op jit(solution)/shard_map/ppermute | solution.py:20
  683.3 11.7 %cholesky.442 = f32[128,128]{1,0:T(8,128)S(1)} custom-call(f32[128,128]{1,0:T(8,128)S(1)} %cholesky.583), custom_call_target="Cholesky" | custom-call | tf_op jit(solution)/shard_map/jit(cholesky)/cholesky | solution.py:96
  705.4 11.7 %cholesky.459 = f32[128,128]{1,0:T(8,128)S(1)} custom-call(f32[128,128]{1,0:T(8,128)S(1)} %slice_subtract_fusion.3), custom_call_target="Cholesky" | custom-call | tf_op jit(solution)/shard_map/jit(cholesky)/cholesky | solution.py:96
  729.0 11.7 %cholesky.476 = f32[128,128]{1,0:T(8,128)S(1)} custom-call(f32[128,128]{1,0:T(8,128)S(1)} %cholesky.586), custom_call_target="Cholesky" | custom-call | tf_op jit(solution)/shard_map/jit(cholesky)/cholesky | solution.py:96
  751.0 11.7 %cholesky.493 = f32[128,128]{1,0:T(8,128)S(1)} custom-call(f32[128,128]{1,0:T(8,128)S(1)} %slice_subtract_fusion.2), custom_call_target="Cholesky" | custom-call | tf_op jit(solution)/shard_map/jit(cholesky)/cholesky | solution.py:96
  768.0 14.1 %collective-permute-done.4 = f32[256,256]{1,0:T(8,128)S(1)} collective-permute-done((f32[256,256]{1,0:T(8,128)S(1)}, f32[256,256]{1,0:T(8,128)S(1)}, u32[]{:S(2)}, u32[]{:S(2)}) %collective-permute-start.4) | collective-permute-done | bytes 262176 | tf_op jit(solution)/shard_map/ppermute | solution.py:20
  782.7 11.7 %cholesky.510 = f32[128,128]{1,0:T(8,128)S(1)} custom-call(f32[128,128]{1,0:T(8,128)S(1)} %cholesky.589), custom_call_target="Cholesky" | custom-call | tf_op jit(solution)/shard_map/jit(cholesky)/cholesky | solution.py:96
  804.8 11.7 %cholesky.527 = f32[128,128]{1,0:T(8,128)S(1)} custom-call(f32[128,128]{1,0:T(8,128)S(1)} %slice_subtract_fusion.1), custom_call_target="Cholesky" | custom-call | tf_op jit(solution)/shard_map/jit(cholesky)/cholesky | solution.py:96
  821.9 13.3 %collective-permute-done.5 = f32[256,256]{1,0:T(8,128)S(1)} collective-permute-done((f32[256,256]{1,0:T(8,128)S(1)}, f32[256,256]{1,0:T(8,128)S(1)}, u32[]{:S(2)}, u32[]{:S(2)}) %collective-permute-start.5) | collective-permute-done | bytes 262176 | tf_op jit(solution)/shard_map/ppermute | solution.py:20
  857.8 11.7 %cholesky.561 = f32[128,128]{1,0:T(8,128)S(1)} custom-call(f32[128,128]{1,0:T(8,128)S(1)} %slice_subtract_fusion), custom_call_target="Cholesky" | custom-call | tf_op jit(solution)/shard_map/jit(cholesky)/cholesky | solution.py:96
  876.8 19.7 %custom-call.12 = f32[2,128,128]{1,2,0:T(8,128)S(1)} custom-call(f32[2,128,128]{2,1,0:T(8,128)S(1)} %get-tuple-element.96), custom_call_target="InvertDiagBlocksLowerTriangular" | custom-call | tf_op jit(solution)/shard_map/jit(_solve_triangular)/triangular_solve | solution.py:97
  (194 shorter events, 233.0 us)
Async XLA Ops:
  7.2 37.8 %all-gather.2.cloned.1.call-start = ((), (), s32[]{:S(2)}) async-start(), calls=%async_computation.1 | async-start | bytes 1179648 | tf_op jit(solution)/shard_map/all_gather | solution.py:84
  7.9 448.0 %reduce-scatter.2.cloned.1.call-start = ((), (), s32[]{:S(2)}) async-start(), calls=%async_computation.2 | async-start | bytes 2359296 | tf_op jit(solution)/shard_map/reduce_scatter | solution.py:88
  49.0 4.0 copy-start.2
  63.9 4.0 copy-start.2
  78.9 4.0 copy-start.2
  89.8 234.9 %copy-start.1 = (s32[96]{0:T(128)S(1)}, s32[96]{0:T(128)}, u32[]{:S(2)}) copy-start(s32[96]{0:T(128)} %get-tuple-element.495) | copy-start | bytes 1156
  89.8 234.9 %copy-start.3 = (s32[96]{0:T(128)S(1)}, s32[96]{0:T(128)}, u32[]{:S(2)}) copy-start(s32[96]{0:T(128)} %get-tuple-element.496) | copy-start | bytes 1156
  372.5 155.6 %all-reduce.4.cloned.1.call-start = ((), (), s32[]{:S(2)}) async-start(), calls=%async_computation.3 | async-start | bytes 262144 | tf_op jit(solution)/shard_map/psum | solution.py:90
  565.9 7.6 collective-permute-start
  610.8 15.9 %collective-permute-start.1 = (f32[256,256]{1,0:T(8,128)S(1)}, f32[256,256]{1,0:T(8,128)S(1)}, u32[]{:S(2)}, u32[]{:S(2)}) collective-permute-start(f32[256,256]{1,0:T(8,128)S(1)} %select_select_fusion.5), channel_id=1, source_target_pairs={{0,2},{2,0},{1,3},{3,1},{4,6},{6,4},{5,7},{7,5},{8,10},{10,8},{9,1... | collective-permute-start | bytes 786440 | tf_op jit(solution)/shard_map/ppermute | solution.py:20
  663.8 18.9 %collective-permute-start.2 = (f32[256,256]{1,0:T(8,128)S(1)}, f32[256,256]{1,0:T(8,128)S(1)}, u32[]{:S(2)}, u32[]{:S(2)}) collective-permute-start(f32[256,256]{1,0:T(8,128)S(1)} %select_select_fusion.4), channel_id=1, source_target_pairs={{0,4},{4,0},{1,5},{5,1},{2,6},{6,2},{3,7},{7,3},{8,12},{12,8},{9,1... | collective-permute-start | bytes 786440 | tf_op jit(solution)/shard_map/ppermute | solution.py:20
  719.9 8.5 collective-permute-start.3
  765.5 16.6 %collective-permute-start.4 = (f32[256,256]{1,0:T(8,128)S(1)}, f32[256,256]{1,0:T(8,128)S(1)}, u32[]{:S(2)}, u32[]{:S(2)}) collective-permute-start(f32[256,256]{1,0:T(8,128)S(1)} %select_select_fusion.2), channel_id=1, source_target_pairs={{0,16},{16,0},{1,17},{17,1},{2,18},{18,2},{3,19},{19,3},{4,20},{20... | collective-permute-start | bytes 786440 | tf_op jit(solution)/shard_map/ppermute | solution.py:20
  819.3 15.9 %collective-permute-start.5 = (f32[256,256]{1,0:T(8,128)S(1)}, f32[256,256]{1,0:T(8,128)S(1)}, u32[]{:S(2)}, u32[]{:S(2)}) collective-permute-start(f32[256,256]{1,0:T(8,128)S(1)} %select_select_fusion.1), channel_id=1, source_target_pairs={{0,32},{32,0},{1,33},{33,1},{2,34},{34,2},{3,35},{35,3},{4,36},{36... | collective-permute-start | bytes 786440 | tf_op jit(solution)/shard_map/ppermute | solution.py:20
  835.6 60.9 %copy-start = (f32[256,256]{1,0:T(8,128)S(1)}, f32[256,256]{1,0:T(8,128)}, u32[]{:S(2)}) copy-start(f32[256,256]{1,0:T(8,128)} %reduce-scatter.2.cloned.1.call-done) | copy-start | bytes 786436
Sparse Core Ops, SparseCore 0:
  10.1 34.7 all-gather.1
  372.6 83.2 reduce-scatter.1
  458.8 69.2 all-reduce.3
where the time goes:
time: 921 us; the launch traced here: 906 us
  other arithmetic  266 us (29%)
  waiting for transfers between devices  252 us (27%)
  blocking collectives  235 us (26%)
  matrix products  80.4 us (9%)
  local copies, waits for them, and re-layouts  24.9 us (3%)
  between operations  24.9 us (3%)
  starting transfers between devices  19 us (2%)
    psum x1, blocking collectives, local(): user_tile = lax.psum(partial_value, 'cols').astype(jnp.bfloat16)  235 us
    another operation x42, other arithmetic, local(): lower = jnp.linalg.cholesky(mine + theirs)  208 us
    reduce_scatter x1, waiting for transfers between devices, local(): lax.psum_scatter(item_terms, 'rows', scatter_dimension=0, tiled=True)  83.1 us
    psum x1, waiting for transfers between devices, local(): lax.psum(gram_local.astype(jnp.bfloat16), 'rows').astype(jnp.float32)  69.9 us
    ppermute x6, waiting for transfers between devices, swapped(): return lax.ppermute(block, axis, route)  62.1 us
    all_gather x1, waiting for transfers between devices, local(): panel = lax.all_gather(start_block, 'rows', axis=0, tiled=True)  36.3 us
    another operation x6, other arithmetic, local(): lower = jnp.linalg.cholesky(gram_rows)  34 us
    dot_general x3, matrix products, backward_step(): jnp.einsum('ni,nbk->ibk', onehot, product, precision=lax.Precision.HIGHEST)  24.8 us
  transfers between devices with their start and end apart: 9, of which 9 were waited for; matrix products, arithmetic and copies ran while one was open for 0% of the time, Pallas kernels for 0%

commit v1 on v0

v1 whole, which is shorter than its diff:
```python
import functools

import jax
import jax.numpy as jnp
from jax import lax
from jax.experimental import pallas as pl
from jax.experimental.pallas import tpu as pltpu
from jax.sharding import PartitionSpec as P

MESH = pl.DeviceIdType.MESH
F32 = jnp.float32
BF16 = jnp.bfloat16
HIGH = lax.Precision.HIGHEST
LIMIT = 48 * 1024 * 1024
NB = 96
GROUP = 8
STEP = 24
X, Y, Z = 4, 8, 8


def vmem():
    return pl.BlockSpec(memory_space=pltpu.VMEM)


def smem():
    return pl.BlockSpec(memory_space=pltpu.SMEM)


def remote(src, dst, send, recv, device):
    return pltpu.make_async_remote_copy(
        src_ref=src, dst_ref=dst, send_sem=send, recv_sem=recv, device_id=device, device_id_type=MESH
    )


def places():
    row = lax.axis_index("rows")
    col = lax.axis_index("cols")
    return row, col, lax.div(col, Z), lax.rem(col, Z)


def each(count, body):
    def step(i, carry):
        body(i)
        return carry

    lax.fori_loop(1, count, step, 0)


def ring(me, i, count):
    return lax.rem(me + i, count)


def greet(makers):
    barrier = pltpu.get_barrier_semaphore()
    total = 0
    for count, device in makers:
        each(
            count,
            lambda i, device=device: pl.semaphore_signal(
                barrier, inc=1, device_id=device(i), device_id_type=MESH
            ),
        )
        total += count - 1
    pl.semaphore_wait(barrier, total)


def gather_kernel(own_ref, out_ref, send, recv):
    row, col, _, _ = places()
    chip, core = lax.div(row, 2), lax.rem(row, 2)
    partner = (chip * 2 + 1 - core, col)

    def peer(i):
        return (ring(chip, i, X) * 2 + core, col)

    barrier = pltpu.get_barrier_semaphore()
    pl.semaphore_signal(barrier, inc=1, device_id=partner, device_id_type=MESH)
    for i in range(1, X):
        pl.semaphore_signal(barrier, inc=1, device_id=peer(i), device_id_type=MESH)
    pl.semaphore_wait(barrier, X)

    sent = []
    for i in (2, 1, 3):
        copy = remote(own_ref, out_ref.at[row], send.at[i], recv.at[i], peer(i))
        copy.start()
        sent.append(copy)
    copy = remote(own_ref, out_ref.at[row], send.at[0], recv.at[0], partner)
    copy.start()
    sent.append(copy)
    out_ref[row] = own_ref[...]
    for i in (1, 3, 2):
        source = ring(chip, X - i, X) * 2 + core
        block = out_ref.at[source]
        remote(own_ref, block, send.at[i], recv.at[i], peer(i)).wait_recv()
        copy = remote(block, block, send.at[X + i], recv.at[X + i], partner)
        copy.start()
        sent.append(copy)
    for i in (0, 1, 3, 2):
        source = ring(chip, X - i, X) * 2 + 1 - core
        j = i if i == 0 else X + i
        remote(own_ref, out_ref.at[source], send.at[j], recv.at[j], partner).wait_recv()
    for copy in sent:
        copy.wait_send()


def gather_panel(own):
    return pl.pallas_call(
        gather_kernel,
        out_shape=jax.ShapeDtypeStruct((8, 256, 256), BF16),
        in_specs=[vmem()],
        out_specs=vmem(),
        scratch_shapes=[pltpu.SemaphoreType.DMA((8,)), pltpu.SemaphoreType.DMA((8,))],
        compiler_params=pltpu.CompilerParams(
            collective_id=0, has_side_effects=True, vmem_limit_bytes=LIMIT
        ),
        name="gather_panel",
    )(own)


def forward_kernel(rows_ref, cols_ref, count_ref, tiles_ref, panel_ref, out_ref, acc_ref):
    step = pl.program_id(0)

    @pl.when(step == 0)
    def _():
        acc_ref[...] = jnp.zeros_like(acc_ref)

    count = count_ref[0]

    def group(g, carry):
        products = []
        for j in range(GROUP):
            at = g * GROUP + j
            slot = step * STEP + at
            tile = jnp.where(slot < count, tiles_ref[at], jnp.zeros((128, 128), BF16))
            products.append(
                jnp.dot(tile, panel_ref[cols_ref[slot]], preferred_element_type=F32)
            )
        for j in range(GROUP):
            slot = step * STEP + g * GROUP + j
            acc_ref[rows_ref[slot]] += products[j]
        return carry

    lax.fori_loop(0, STEP // GROUP, group, 0)

    @pl.when(step == NB // STEP - 1)
    def _():
        for u in range(8):
            for h in range(2):
                out_ref[h, u] = acc_ref[u, :, h * 128 : (h + 1) * 128].astype(BF16)


def backward_kernel(rows_ref, cols_ref, count_ref, tiles_ref, users_ref, out_ref, wide_ref):
    step = pl.program_id(0)

    @pl.when(step == 0)
    def _():
        out_ref[...] = jnp.zeros_like(out_ref)
        for u in range(8):
            for h in range(2):
                wide_ref[u, :, h * 128 : (h + 1) * 128] = users_ref[h, u]

    count = count_ref[0]

    def group(g, carry):
        products = []
        for j in range(GROUP):
            at = g * GROUP + j
            slot = step * STEP + at
            tile = jnp.where(slot < count, tiles_ref[at], jnp.zeros((128, 128), BF16))
            products.append(
                lax.dot_general(
                    tile, wide_ref[rows_ref[slot]], (((0,), (0,)), ((), ())), preferred_element_type=F32
                )
            )
        for j in range(GROUP):
            slot = step * STEP + g * GROUP + j
            out_ref[cols_ref[slot]] += products[j]
        return carry

    lax.fori_loop(0, STEP // GROUP, group, 0)


def sparse_call(kernel, rows, cols, count, tiles, operand, out, scratch, name):
    zeros = (0,) * operand.ndim
    zeros_out = (0,) * len(out.shape)
    return pl.pallas_call(
        kernel,
        grid=(NB // STEP,),
        out_shape=out,
        in_specs=[
            smem(),
            smem(),
            smem(),
            pl.BlockSpec((STEP, 128, 128), lambda i: (i, 0, 0)),
            pl.BlockSpec(operand.shape, lambda i: zeros),
        ],
        out_specs=pl.BlockSpec(out.shape, lambda i: zeros_out),
        scratch_shapes=[scratch],
        compiler_params=pltpu.CompilerParams(
            dimension_semantics=("arbitrary",), vmem_limit_bytes=LIMIT
        ),
        name=name,
    )(rows, cols, count, tiles, operand)


def users_kernel(part_ref, out_ref, got1, sum1, got2, mine, wide, send, recv):
    row, col, y, z = places()
    me = (y, z)

    def along(axis, i):
        if axis == 0:
            return ring(y, i, Y), (row, ring(y, i, Y) * Z + z)
        return ring(z, i, Z), (row, y * Z + ring(z, i, Z))

    greet([(Y, lambda i: along(0, i)[1]), (Z, lambda i: along(1, i)[1])])

    def exchange(stage, jobs):
        for half, (axis, source, landing) in enumerate(jobs):
            def start(i, half=half, axis=axis, source=source, landing=landing):
                target, device = along(axis, i)
                remote(
                    source(target), landing.at[me[axis]],
                    send.at[stage, half, i], recv.at[stage, half, i], device,
                ).start()

            each(8, start)

    def arrived(stage, jobs):
        for half, (axis, source, landing) in enumerate(jobs):
            def wait(i, half=half, axis=axis, source=source, landing=landing):
                origin = ring(me[axis], 8 - i, 8)
                target, device = along(axis, i)
                remote(
                    source(target), landing.at[origin],
                    send.at[stage, half, i], recv.at[stage, half, i], device,
                ).wait_recv()

            each(8, wait)

    def departed(stage, jobs):
        for half, (axis, source, landing) in enumerate(jobs):
            def wait(i, half=half, axis=axis, source=source, landing=landing):
                target, device = along(axis, i)
                remote(
                    source(target), landing.at[me[axis]],
                    send.at[stage, half, i], recv.at[stage, half, i], device,
                ).wait_send()

            each(8, wait)

    first = [(h, lambda t, h=h: part_ref.at[h, t], got1.at[h]) for h in range(2)]
    exchange(0, first)
    for h in range(2):
        got1[h, me[h]] = part_ref[h, me[h]]
    arrived(0, first)
    for h in range(2):
        total = got1[h, 0].astype(F32)
        for k in range(1, 8):
            total = total + got1[h, k].astype(F32)
        sum1[h] = total.reshape(8, 16, 128)

    second = [(1 - h, lambda t, h=h: sum1.at[h, t], got2.at[h]) for h in range(2)]
    exchange(1, second)
    for h in range(2):
        got2[h, me[1 - h]] = sum1[h, me[1 - h]]
    arrived(1, second)
    for h in range(2):
        total = got2[h, 0]
        for k in range(1, 8):
            total = total + got2[h, k]
        mine[h] = total.astype(BF16)

    third = [(1 - h, lambda t, h=h: mine.at[h], wide.at[h]) for h in range(2)]
    exchange(2, third)
    for h in range(2):
        wide[h, me[1 - h]] = mine[h]
    arrived(2, third)

    fourth = [(h, lambda t, h=h: wide.at[h], out_ref.at[h]) for h in range(2)]
    exchange(3, fourth)
    for h in range(2):
        out_ref[h, me[h]] = wide[h]
    arrived(3, fourth)
    for stage, jobs in enumerate((first, second, third, fourth)):
        departed(stage, jobs)


def sum_users(part):
    return pl.pallas_call(
        users_kernel,
        out_shape=jax.ShapeDtypeStruct((2, 8, 8, 16, 128), BF16),
        in_specs=[vmem()],
        out_specs=vmem(),
        scratch_shapes=[
            pltpu.VMEM((2, 8, 128, 128), BF16),
            pltpu.VMEM((2, 8, 16, 128), F32),
            pltpu.VMEM((2, 8, 16, 128), F32),
            pltpu.VMEM((2, 16, 128), BF16),
            pltpu.VMEM((2, 8, 16, 128), BF16),
            pltpu.SemaphoreType.DMA((4, 2, 8)),
            pltpu.SemaphoreType.DMA((4, 2, 8)),
        ],
        compiler_params=pltpu.CompilerParams(
            collective_id=1, has_side_effects=True, vmem_limit_bytes=LIMIT
        ),
        name="sum_users",
    )(part)


def items_kernel(
    terms_ref, items_ref, gram_ref, near, pack, far, cut, got1, sum1, got2, sum2, got3, sum3, wide,
    send_a, recv_a, send_b, recv_b, send, recv,
):
    row, col, y, z = places()
    chip, core = lax.div(row, 2), lax.rem(row, 2)
    partner = (chip * 2 + 1 - core, col)
    spots = {"r": row, "y": y, "z": z}

    def along(axis, i):
        target = ring(spots[axis], i, 8)
        if axis == "r":
            return target, (target, col)
        if axis == "y":
            return target, (row, target * Z + z)
        return target, (row, y * Z + target)

    greet([(8, lambda i, axis=axis: along(axis, i)[1]) for axis in "ryz"])

    close = []
    for i in (1, 3, 2, 0):
        chunk = ring(chip, i, X) * 2 + 1 - core
        copy = remote(terms_ref.at[chunk], near.at[i], send_a.at[i], recv_a.at[i], partner)
        copy.start()
        close.append(copy)
    hops = []
    for n, i in enumerate((1, 3, 2)):
        close[n].wait_recv()
        chunk = ring(chip, i, X) * 2 + core
        pack[i] = (terms_ref[chunk] + near[i]).astype(BF16)
        copy = remote(pack.at[i], far.at[i], send_b.at[i], recv_b.at[i], (chunk, col))
        copy.start()
        hops.append(copy)
    close[3].wait_recv()
    items = terms_ref[row] + near[0]
    for n, i in enumerate((1, 3, 2)):
        hops[n].wait_recv()
        items = items + far[i].astype(F32)
    items_ref[...] = items

    gram = lax.dot_general(
        items, items, (((0,), (0,)), ((), ())), precision=HIGH, preferred_element_type=F32
    )
    for k in range(32):
        for c in range(2):
            cut[k // 4, (k % 4) * 2 + c] = gram[8 * k : 8 * k + 8, 128 * c : 128 * c + 128]

    def move(stage, axis, source, landing):
        here = spots[axis]

        def start(i):
            target, device = along(axis, i)
            remote(
                source(target), landing.at[here], send.at[stage, i], recv.at[stage, i], device
            ).start()

        def wait(i):
            target, device = along(axis, i)
            remote(
                source(target), landing.at[ring(here, 8 - i, 8)], send.at[stage, i], recv.at[stage, i], device
            ).wait_recv()

        each(8, start)
        landing[here] = source(here)[...]
        each(8, wait)

    def left(stage, axis, source, landing):
        def wait(i):
            target, device = along(axis, i)
            remote(
                source(target), landing.at[spots[axis]], send.at[stage, i], recv.at[stage, i], device
            ).wait_send()

        each(8, wait)

    def summed(got):
        total = got[0]
        for k in range(1, 8):
            total = total + got[k]
        return total

    jobs = [
        ("r", lambda t: cut.at[t], got1),
        ("y", lambda t: sum1.at[t], got2),
        ("z", lambda t: sum2, got3),
        ("y", lambda t: sum3, wide),
        ("r", lambda t: wide, gram_ref),
    ]
    move(0, *jobs[0])
    sum1[...] = summed(got1)
    move(1, *jobs[1])
    sum2[...] = summed(got2)
    move(2, *jobs[2])
    sum3[...] = summed(got3)
    move(3, *jobs[3])
    move(4, *jobs[4])
    for copy in close + hops:
        copy.wait_send()
    for stage, job in enumerate(jobs):
        left(stage, *job)


def sum_items(terms):
    tile = (8, 128)
    return pl.pallas_call(
        items_kernel,
        out_shape=(
            jax.ShapeDtypeStruct((256, 256), F32),
            jax.ShapeDtypeStruct((8, 8) + tile, F32),
        ),
        in_specs=[vmem()],
        out_specs=(vmem(), vmem()),
        scratch_shapes=[
            pltpu.VMEM((X, 256, 256), F32),
            pltpu.VMEM((X, 256, 256), BF16),
            pltpu.VMEM((X, 256, 256), BF16),
            pltpu.VMEM((8, 8) + tile, F32),
            pltpu.VMEM((8, 8) + tile, F32),
            pltpu.VMEM((8,) + tile, F32),
            pltpu.VMEM((8,) + tile, F32),
            pltpu.VMEM(tile, F32),
            pltpu.VMEM((8,) + tile, F32),
            pltpu.VMEM(tile, F32),
            pltpu.VMEM((8,) + tile, F32),
            pltpu.SemaphoreType.DMA((X,)),
            pltpu.SemaphoreType.DMA((X,)),
            pltpu.SemaphoreType.DMA((X,)),
            pltpu.SemaphoreType.DMA((X,)),
            pltpu.SemaphoreType.DMA((5, 8)),
            pltpu.SemaphoreType.DMA((5, 8)),
        ],
        compiler_params=pltpu.CompilerParams(
            collective_id=2, has_side_effects=True, vmem_limit_bytes=LIMIT
        ),
        name="sum_items",
    )(terms)


PANEL = 32
N = 256


def factor_kernel(gram_ref, items_ref, basis_ref, factor_ref, a_ref, d_ref):
    for k in range(32):
        for c in range(2):
            a_ref[8 * k : 8 * k + 8, 128 * c : 128 * c + 128] = gram_ref[k // 4, (k % 4) * 2 + c]

    def panel(q, carry):
        base = q * PANEL
        rows = pl.ds(pl.multiple_of(base, PANEL), PANEL)
        w = pltpu.roll(a_ref[rows, :], lax.rem(N - base, N), 1)
        d = jnp.zeros((PANEL, 128), F32)
        for t in range(PANEL // 8):
            low = 8 * t
            part = w[low:, :]
            size = PANEL - low
            lane = lax.broadcasted_iota(jnp.int32, (size, N), 1)
            sub = lax.broadcasted_iota(jnp.int32, (size, N), 0) + low
            sub1 = sub[:, :128]
            columns = [
                jnp.broadcast_to(part[:, low + b : low + b + 1], (size, 128)) for b in range(8)
            ]
            d_part = d[low:, :]
            for a in range(8):
                r = low + a
                pivot = columns[a][a : a + 1, :]
                m = jnp.where(sub1 > r, columns[a] * (1.0 / pivot), 0.0)
                for b in range(a + 1, 8):
                    columns[b] = columns[b] - m * columns[b][a : a + 1, :]
                line = jnp.where(lane[:1] == r, 1.0, part[a : a + 1, :])
                kept = jnp.where((lane == r) & (sub > r), 0.0, part)
                part = kept - jnp.concatenate([m, m], axis=1) * line
                d_part = jnp.where(sub1 == r, pivot, d_part)
            w = part if low == 0 else jnp.concatenate([w[:low], part], axis=0)
            d = d_part if low == 0 else jnp.concatenate([d[:low], d_part], axis=0)
        d_ref[rows, :] = d
        lane = lax.broadcasted_iota(jnp.int32, (PANEL, N), 1)
        sub = lax.broadcasted_iota(jnp.int32, (PANEL, N), 0)
        d2 = jnp.concatenate([d, d], axis=1)
        ahead = (lane >= PANEL) & (lane < N - base)
        scaled = jnp.where(ahead, w / d2, 0.0)
        right = jnp.where((lane < PANEL) & (lane >= sub), jnp.where(lane == sub, 1.0, 0.0), w)
        a_ref[rows, :] = pltpu.roll(w, base, 1)
        scaled = pltpu.roll(scaled, base, 1)
        right = pltpu.roll(right, base, 1)
        update = lax.dot_general(
            scaled, right, (((0,), (0,)), ((), ())), precision=HIGH, preferred_element_type=F32
        )
        full_lane = lax.broadcasted_iota(jnp.int32, (N, N), 1)
        full_sub = lax.broadcasted_iota(jnp.int32, (N, N), 0)
        done = (full_sub >= base + PANEL) & (full_lane >= base) & (full_lane < base + PANEL)
        a_ref[...] = jnp.where(done, 0.0, a_ref[...]) - update
        return carry

    lax.fori_loop(0, N // PANEL, panel, 0)

    lane = lax.broadcasted_iota(jnp.int32, (N, N), 1)
    sub = lax.broadcasted_iota(jnp.int32, (N, N), 0)
    scale = 1.0 / jnp.sqrt(d_ref[...])
    scale = jnp.concatenate([scale, scale], axis=1)
    full = a_ref[...]
    factor_ref[...] = jnp.where(lane >= sub, full, 0.0) * scale
    inverse = jnp.where(lane < sub, full, jnp.where(lane == sub, 1.0, 0.0)) * scale
    basis_ref[...] = lax.dot_general(
        items_ref[...], inverse, (((1,), (1,)), ((), ())), precision=HIGH, preferred_element_type=F32
    )


def factor_call(gram, items):
    return pl.pallas_call(
        factor_kernel,
        out_shape=(
            jax.ShapeDtypeStruct((256, 256), F32),
            jax.ShapeDtypeStruct((256, 256), F32),
        ),
        in_specs=[vmem(), vmem()],
        out_specs=(vmem(), vmem()),
        scratch_shapes=[pltpu.VMEM((N, N), F32), pltpu.VMEM((N, 128), F32)],
        compiler_params=pltpu.CompilerParams(vmem_limit_bytes=LIMIT),
        name="factor",
    )(gram, items)


def local(blocks, block_row, block_col, counts, start_block):
    tiles = blocks[0, 0]
    rows = block_row[0, 0]
    cols = block_col[0, 0]
    count = counts[0]
    panel = gather_panel(start_block).reshape(16, 128, 256)
    part = sparse_call(
        forward_kernel, rows, cols, count, tiles, panel,
        jax.ShapeDtypeStruct((2, 8, 128, 128), BF16), pltpu.VMEM((8, 128, 256), F32), "forward",
    )
    users = sum_users(part).reshape(2, 8, 128, 128)
    terms = sparse_call(
        backward_kernel, rows, cols, count, tiles, users,
        jax.ShapeDtypeStruct((16, 128, 256), F32), pltpu.VMEM((8, 128, 256), BF16), "backward",
    )
    items, gram = sum_items(terms.reshape(8, 256, 256))
    return factor_call(gram, items)


def solution(mesh):
    return jax.shard_map(
        local,
        mesh=mesh,
        in_specs=(
            P("rows", "cols", None, None, None),
            P("rows", "cols", None),
            P("rows", "cols", None),
            P("rows", "cols"),
            P(("cols", "rows"), None),
        ),
        out_specs=(P(("cols", "rows"), None), P()),
        check_vma=False,
    )
```

time: 921 us -> 120 us (0.13); the launches traced: 906 us -> 120 us
  other arithmetic: 266 us -> 0 us
  waiting for transfers between devices: 252 us -> 0 us
  blocking collectives: 235 us -> 0 us
  Pallas kernels: 0 us -> 114 us
  matrix products: 80.4 us -> 0 us
  between operations: 24.9 us -> 1.36 us
  local copies, waits for them, and re-layouts: 24.9 us -> 4.11 us
  starting transfers between devices: 19 us -> 0 us
    another operation x50 -> x0, other arithmetic: 262 us -> none  [the longest x42 208 us: local(): lower = jnp.linalg.cholesky(mine + theirs)]
    psum x1 -> x0, blocking collectives: 235 us -> none  [local(): user_tile = lax.psum(partial_value, 'cols').astype(jnp.bfloat16)]
    pallas_call x0 -> x6, Pallas kernels: none -> 114 us  [the longest x1 40.9 us: sum_items(): pl.pallas_call(items_kernel, out_shape=(jax.ShapeDtypeStruct((256, 256),...]
    reduce_scatter x1 -> x0, waiting for transfers between devices: 83.1 us -> none  [local(): lax.psum_scatter(item_terms, 'rows', scatter_dimension=0, tiled=True)]
    dot_general x25 -> x0, matrix products: 76.1 us -> none  [the longest x3 24.8 us: backward_step(): jnp.einsum('ni,nbk->ibk', onehot, product, precision=lax.Precision.HIGHEST)]
    psum x1 -> x0, waiting for transfers between devices: 69.9 us -> none  [local(): lax.psum(gram_local.astype(jnp.bfloat16), 'rows').astype(jnp.float32)]
    ppermute x6 -> x0, waiting for transfers between devices: 62.1 us -> none  [swapped(): return lax.ppermute(block, axis, route)]
    all_gather x1 -> x0, waiting for transfers between devices: 36.3 us -> none  [local(): panel = lax.all_gather(start_block, 'rows', axis=0, tiled=True)]
  transfers between devices with their start and end apart: 9 -> 0, of which waited for: 9 -> 0; matrix products, arithmetic and copies ran while one was open for 0% -> 0% of each run, Pallas kernels for 0% -> 0%
where the time goes in v1:
time: 120 us
  Pallas kernels  114 us (95%)
  local copies, waits for them, and re-layouts  4.11 us (3%)
  between operations  1.36 us (1%)
    pallas_call x1, Pallas kernels, sum_items(): pl.pallas_call(items_kernel, out_shape=(jax.ShapeDtypeStruct((256, 256),...  40.9 us
    pallas_call x1, Pallas kernels, sum_users(): pl.pallas_call(users_kernel, out_shape=jax.ShapeDtypeStruct((2, 8, 8, 16,...  35.7 us
    pallas_call x1, Pallas kernels, gather_panel(): pl.pallas_call(gather_kernel, out_shape=jax.ShapeDtypeStruct((8, 256, 256...  16.6 us
    pallas_call x1, Pallas kernels, factor_call(): pl.pallas_call(factor_kernel, out_shape=(jax.ShapeDtypeStruct((256, 256),...  11.9 us
    pallas_call x2, Pallas kernels, sparse_call(): pl.pallas_call(kernel, grid=(NB // STEP,), out_shape=out, in_specs=[smem(...  9.42 us
    unnamed x12, local copies, waits for them, and re-layouts  4.11 us

profile of v1, /device:TPU:1, one launch (start us, length us, event | category | flops | bytes accessed | tf_op | source)
XLA Modules:
  0.0 119.9 jit_solution(374764880841588597)
XLA Ops:
  1.3 0.0 copy-start.2
  1.3 0.9 copy-done.2
  2.2 16.6 %gather_panel.1 = bf16[8,256,256]{2,1,0:T(8,128)(2,1)S(1)} custom-call(bf16[256,256]{1,0:T(8,128)(2,1)S(1)} %copy-done.2), custom_call_target="tpu_custom_call" | custom-call | tf_op jit(solution)/shard_map/gather_panel/pallas_call | solution.py:106
  18.8 0.0 copy-start.4
  18.8 0.0 copy-start
  18.8 1.9 %copy-done = bf16[1,1,96,128,128]{4,3,2,1,0:T(8,128)(2,1)S(1)} copy-done((bf16[1,1,96,128,128]{4,3,2,1,0:T(8,128)(2,1)S(1)}, bf16[1,1,96,128,128]{4,3,2,1,0:T(8,128)(2,1)}, u32[]{:S(2)}) %copy-start) | copy-done | bytes 3145752
  20.7 0.0 copy-start.3
  20.7 0.7 copy-done.3
  21.3 0.0 copy-start.5
  21.3 0.7 copy-done.5
  22.0 0.0 copy-start.1
  22.0 4.4 %forward.1.part_ref = bf16[2,8,128,128]{3,2,1,0:T(8,128)(2,1)S(1)} custom-call(s32[96]{0:T(128)S(1)} %bitcast.14, s32[96]{0:T(128)S(1)} %bitcast.16, s32[1]{0:T(128)} %bitcast.7.count_ref, bf16[96,128,128]{2,1,0:T(8,128)(2,1)S(1)} %bitcast.9, bf16[16,128,256]{2,1,0:T(8,128)(2,1)S(1)} %bitcast.12), custom_call_target="tpu_custom_call" | custom-call | tf_op jit(solution)/shard_map/forward/pallas_call | solution.py:185
  26.4 35.7 %sum_users.1 = bf16[2,8,8,16,128]{4,3,2,1,0:T(8,128)(2,1)S(1)} custom-call(bf16[2,8,128,128]{3,2,1,0:T(8,128)(2,1)S(1)} %forward.1.part_ref), custom_call_target="tpu_custom_call" | custom-call | tf_op jit(solution)/shard_map/sum_users/pallas_call | solution.py:288
  62.0 0.0 copy-done.4
  62.1 0.0 copy-done.1
  62.1 5.0 %backward.1 = f32[16,128,256]{2,1,0:T(8,128)S(1)} custom-call(s32[96]{0:T(128)S(1)} %bitcast.15, s32[96]{0:T(128)S(1)} %bitcast.17, s32[1]{0:T(128)} %bitcast.8.count_ref, bf16[96,128,128]{2,1,0:T(8,128)(2,1)S(1)} %bitcast.10, bf16[2,8,128,128]{3,2,1,0:T(8,128)(2,1)S(1)} %bitcast.13), custom_call_target="tpu_custom_call" | custom-call | tf_op jit(solution)/shard_map/backward/pallas_call | solution.py:185
  67.1 40.9 %sum_items.1 = (f32[256,256]{1,0:T(8,128)S(1)}, f32[8,8,8,128]{3,2,1,0:T(8,128)S(1)}) custom-call(f32[8,256,256]{2,1,0:T(8,128)S(1)} %bitcast.11), custom_call_target="tpu_custom_call" | custom-call | tf_op jit(solution)/shard_map/sum_items/pallas_call | solution.py:413
  108.0 11.9 %factor.1 = (f32[256,256]{1,0:T(8,128)}, f32[256,256]{1,0:T(8,128)}) custom-call(f32[8,8,8,128]{3,2,1,0:T(8,128)S(1)} %get-tuple-element.4.gram_ref, f32[256,256]{1,0:T(8,128)S(1)} %get-tuple-element.5.items_ref), custom_call_target="tpu_custom_call" | custom-call | tf_op jit(solution)/shard_map/factor/pallas_call | solution.py:518
Async XLA Ops:
  1.3 0.9 copy-start.2
  18.8 43.3 %copy-start.4 = (s32[1,1,96]{2,1,0:T(1,128)S(1)}, s32[1,1,96]{2,1,0:T(1,128)}, u32[]{:S(2)}) copy-start(s32[1,1,96]{2,1,0:T(1,128)} %param.6) | copy-start | bytes 1156
  18.8 1.9 %copy-start = (bf16[1,1,96,128,128]{4,3,2,1,0:T(8,128)(2,1)S(1)}, bf16[1,1,96,128,128]{4,3,2,1,0:T(8,128)(2,1)}, u32[]{:S(2)}) copy-start(bf16[1,1,96,128,128]{4,3,2,1,0:T(8,128)(2,1)} %param.5) | copy-start | bytes 9437188
  20.7 0.7 copy-start.3
  21.3 0.7 copy-start.5
  22.0 40.1 %copy-start.1 = (bf16[1,1,96,128,128]{4,3,2,1,0:T(8,128)(2,1)S(1)}, bf16[1,1,96,128,128]{4,3,2,1,0:T(8,128)(2,1)}, u32[]{:S(2)}) copy-start(bf16[1,1,96,128,128]{4,3,2,1,0:T(8,128)(2,1)} %param.5) | copy-start | bytes 9437188

commit v2 on v0

v2 whole, which is shorter than its diff:
```python
import jax
import jax.numpy as jnp
from jax import lax
from jax.experimental import pallas as pl
from jax.experimental.pallas import tpu as pltpu
from jax.sharding import PartitionSpec as P

MESH = pl.DeviceIdType.MESH
F32 = jnp.float32
BF16 = jnp.bfloat16
HIGH = lax.Precision.HIGHEST
LIMIT = 48 * 1024 * 1024
NB = 96
GROUP = 8
STEP = 24
X, Y, Z = 4, 8, 8


def vmem():
    return pl.BlockSpec(memory_space=pltpu.VMEM)


def smem():
    return pl.BlockSpec(memory_space=pltpu.SMEM)


def remote(src, dst, send, recv, device):
    return pltpu.make_async_remote_copy(
        src_ref=src, dst_ref=dst, send_sem=send, recv_sem=recv, device_id=device, device_id_type=MESH
    )


def places():
    row = lax.axis_index("rows")
    col = lax.axis_index("cols")
    return row, col, lax.div(col, Z), lax.rem(col, Z)


def each(count, body):
    def step(i, carry):
        body(i)
        return carry

    lax.fori_loop(1, count, step, 0)


def ring(me, i, count):
    return lax.rem(me + i, count)


def greet(makers):
    barrier = pltpu.get_barrier_semaphore()
    total = 0
    for count, device in makers:
        each(
            count,
            lambda i, device=device: pl.semaphore_signal(
                barrier, inc=1, device_id=device(i), device_id_type=MESH
            ),
        )
        total += count - 1
    pl.semaphore_wait(barrier, total)


def dense_kernel(rows_ref, cols_ref, count_ref, tiles_ref, out_ref, acc_ref):
    step = pl.program_id(0)

    @pl.when(step == 0)
    def _():
        acc_ref[...] = jnp.zeros_like(acc_ref)

    count = count_ref[0]

    def group(g, carry):
        for j in range(GROUP):
            at = g * GROUP + j
            slot = step * STEP + at
            tile = jnp.where(slot < count, tiles_ref[at].astype(F32), 0.0)
            place = cols_ref[slot]
            acc_ref[lax.div(place, 2), lax.rem(place, 2), rows_ref[slot]] += tile
        return carry

    lax.fori_loop(0, STEP // GROUP, group, 0)

    @pl.when(step == NB // STEP - 1)
    def _():
        def chunk(q, carry):
            for u in range(8):
                for e in range(2):
                    out_ref[q, u * 128 : (u + 1) * 128, e * 128 : (e + 1) * 128] = acc_ref[
                        q, e, u
                    ].astype(BF16)
            return carry

        lax.fori_loop(0, 8, chunk, 0)


def dense_tile(rows, cols, count, tiles):
    return pl.pallas_call(
        dense_kernel,
        grid=(NB // STEP,),
        out_shape=jax.ShapeDtypeStruct((8, 1024, 256), BF16),
        in_specs=[smem(), smem(), smem(), pl.BlockSpec((STEP, 128, 128), lambda i: (i, 0, 0))],
        out_specs=pl.BlockSpec((8, 1024, 256), lambda i: (0, 0, 0)),
        scratch_shapes=[pltpu.VMEM((8, 2, 8, 128, 128), F32)],
        compiler_params=pltpu.CompilerParams(
            dimension_semantics=("arbitrary",), vmem_limit_bytes=LIMIT
        ),
        name="dense_tile",
    )(rows, cols, count, tiles)


HALF = 128


def krylov_kernel(
    own_ref, tile_ref, items_ref, gram_ref,
    panel, acc, part, got1, sum1, got2, mine, wide, turned, users,
    give, near, pack, relay, far, cut, gram1, gsum1, gram2, gsum2, gram3, gsum3, gwide,
    send_p, recv_p, send_u, recv_u, send_a, recv_a, send_b, recv_b, send_g, recv_g,
):
    row, col, y, z = places()
    chip, core = lax.div(row, 2), lax.rem(row, 2)
    other = 1 - core
    partner = (chip * 2 + other, col)
    spots = {"r": row, "y": y, "z": z}

    def spot(i, which):
        return ring(chip, i, X) * 2 + which

    def beside(i):
        return (spot(i, core), col)

    def along(axis, i):
        target = ring(spots[axis], i, 8)
        if axis == "r":
            return target, (target, col)
        if axis == "y":
            return target, (row, target * Z + z)
        return target, (row, y * Z + target)

    greet([(8, lambda i, axis=axis: along(axis, i)[1]) for axis in "ryz"])

    sent = []

    def push(n, src, dst, device):
        copy = remote(src, dst, send_p.at[n], recv_p.at[n], device)
        copy.start()
        sent.append(copy)

    def landed(n, dst):
        remote(dst, dst, send_p.at[n], recv_p.at[n], partner).wait_recv()

    def product(q):
        return jnp.dot(tile_ref[q], panel[q], preferred_element_type=F32)

    push(1, own_ref, panel.at[row], beside(1))
    push(2, own_ref, panel.at[row], beside(3))
    push(0, own_ref, panel.at[row], partner)
    acc[...] = jnp.dot(tile_ref[row], own_ref[...], preferred_element_type=F32)
    landed(0, panel.at[spot(0, other)])
    acc[...] += product(spot(0, other))
    low, high = pl.ds(0, HALF), pl.ds(HALF, HALF)
    prev, nxt, over = spot(3, core), spot(1, core), spot(2, core)
    landed(1, panel.at[prev])
    push(3, panel.at[prev, low], panel.at[prev, low], beside(1))
    push(5, panel.at[prev], panel.at[prev], partner)
    landed(2, panel.at[nxt])
    push(4, panel.at[nxt, high], panel.at[nxt, high], beside(3))
    push(6, panel.at[nxt], panel.at[nxt], partner)
    acc[...] += product(prev)
    acc[...] += product(nxt)
    landed(5, panel.at[spot(3, other)])
    acc[...] += product(spot(3, other))
    landed(6, panel.at[spot(1, other)])
    acc[...] += product(spot(1, other))
    landed(3, panel.at[over, low])
    push(7, panel.at[over, low], panel.at[over, low], partner)
    landed(4, panel.at[over, high])
    push(8, panel.at[over, high], panel.at[over, high], partner)
    acc[...] += product(over)
    last = spot(2, other)
    landed(7, panel.at[last, low])
    landed(8, panel.at[last, high])
    total = acc[...] + product(last)
    for u in range(8):
        for h in range(2):
            part[h, u] = total[u * 128 : (u + 1) * 128, h * 128 : (h + 1) * 128].astype(BF16)

    def walk(axis, source, landing, sends, recvs, what):
        here = spots[axis]

        def step(i):
            target, device = along(axis, i)
            place = here if what != "arrive" else ring(here, 8 - i, 8)
            copy = remote(source(target), landing.at[place], sends.at[i], recvs.at[i], device)
            if what == "start":
                copy.start()
            elif what == "arrive":
                copy.wait_recv()
            else:
                copy.wait_send()

        each(8, step)

    stages = []

    def exchange(jobs):
        stage = len(stages)
        stages.append(jobs)
        for h, job in enumerate(jobs):
            walk(*job, send_u.at[stage, h], recv_u.at[stage, h], "start")

    def arrived(h):
        stage = len(stages) - 1
        walk(*stages[stage][h], send_u.at[stage, h], recv_u.at[stage, h], "arrive")

    me, first, second = (y, z), ("y", "z"), ("z", "y")
    exchange([(first[h], lambda t, h=h: part.at[h, t], got1.at[h]) for h in range(2)])
    for h in range(2):
        got1[h, me[h]] = part[h, me[h]]
    for h in range(2):
        arrived(h)
        total = got1[h, 0].astype(F32)
        for k in range(1, 8):
            total = total + got1[h, k].astype(F32)
        sum1[h] = total.reshape(8, 16, 128)
    exchange([(second[h], lambda t, h=h: sum1.at[h, t], got2.at[h]) for h in range(2)])
    for h in range(2):
        got2[h, me[1 - h]] = sum1[h, me[1 - h]]
    for h in range(2):
        arrived(h)
        total = got2[h, 0]
        for k in range(1, 8):
            total = total + got2[h, k]
        mine[h] = total.astype(BF16)
    exchange([(second[h], lambda t, h=h: mine.at[h], wide.at[h]) for h in range(2)])
    for h in range(2):
        wide[h, me[1 - h]] = mine[h]
    for h in range(2):
        arrived(h)
        turned[h] = wide[h].reshape(128, 128).astype(F32).T.astype(BF16)
    exchange([(first[h], lambda t, h=h: turned.at[h], users.at[h]) for h in range(2)])
    for h in range(2):
        users[h, me[h]] = turned[h]
    for h in range(2):
        arrived(h)

    def term(q):
        left = jnp.concatenate(
            [jnp.concatenate([users[h, u] for u in range(8)], axis=1) for h in range(2)], axis=0
        )
        return jnp.dot(left, tile_ref[q], preferred_element_type=F32)

    def start(n, src, dst, device):
        copy = remote(src, dst, send_b.at[n], recv_b.at[n], device)
        copy.start()
        sent.append(copy)

    def met(n, dst):
        remote(dst, dst, send_b.at[n], recv_b.at[n], partner).wait_recv()

    close = {}
    for i in (2, 1, 3, 0):
        give[i] = term(spot(i, other))
        close[i] = remote(give.at[i], near.at[i], send_a.at[i], recv_a.at[i], partner)
        close[i].start()
        sent.append(close[i])

    t2 = term(spot(2, core))
    close[2].wait_recv()
    pack[2] = (t2 + near[2]).astype(BF16)
    start(0, pack.at[2, low], relay.at[0], beside(1))
    start(1, pack.at[2, high], relay.at[1], beside(3))
    t1 = term(spot(1, core))
    close[1].wait_recv()
    near[1] = t1 + near[1]
    pack[1, HALF:] = near[1, HALF:].astype(BF16)
    start(2, pack.at[1, high], far.at[0, high], beside(1))
    t3 = term(spot(3, core))
    close[3].wait_recv()
    near[3] = t3 + near[3]
    pack[3, :HALF] = near[3, :HALF].astype(BF16)
    start(3, pack.at[3, low], far.at[1, low], beside(3))
    t0 = term(row)
    close[0].wait_recv()
    near[0] = t0 + near[0]
    met(0, relay.at[0])
    pack[1, :HALF] = (near[1, :HALF] + relay[0].astype(F32)).astype(BF16)
    start(4, pack.at[1, low], far.at[0, low], beside(1))
    met(1, relay.at[1])
    pack[3, HALF:] = (near[3, HALF:] + relay[1].astype(F32)).astype(BF16)
    start(5, pack.at[3, high], far.at[1, high], beside(3))
    met(2, far.at[0, high])
    met(3, far.at[1, low])
    met(4, far.at[0, low])
    met(5, far.at[1, high])
    items = near[0] + far[0].astype(F32) + far[1].astype(F32)
    items_ref[...] = items

    gram = lax.dot_general(
        items, items, (((1,), (1,)), ((), ())), precision=HIGH, preferred_element_type=F32
    )
    for k in range(32):
        for c in range(2):
            cut[k // 4, (k % 4) * 2 + c] = gram[8 * k : 8 * k + 8, 128 * c : 128 * c + 128]

    def summed(got):
        total = got[0]
        for k in range(1, 8):
            total = total + got[k]
        return total

    jobs = [
        ("r", lambda t: cut.at[t], gram1),
        ("y", lambda t: gsum1.at[t], gram2),
        ("z", lambda t: gsum2, gram3),
        ("y", lambda t: gsum3, gwide),
        ("r", lambda t: gwide, gram_ref),
    ]

    def move(n):
        axis, source, landing = jobs[n]
        walk(*jobs[n], send_g.at[n], recv_g.at[n], "start")
        landing[spots[axis]] = source(spots[axis])[...]
        walk(*jobs[n], send_g.at[n], recv_g.at[n], "arrive")

    move(0)
    gsum1[...] = summed(gram1)
    move(1)
    gsum2[...] = summed(gram2)
    move(2)
    gsum3[...] = summed(gram3)
    move(3)
    move(4)

    for copy in sent:
        copy.wait_send()
    for stage, pair in enumerate(stages):
        for h, job in enumerate(pair):
            walk(*job, send_u.at[stage, h], recv_u.at[stage, h], "leave")
    for n, job in enumerate(jobs):
        walk(*job, send_g.at[n], recv_g.at[n], "leave")


def krylov(own, tile):
    cell = (8, 128)
    dma = pltpu.SemaphoreType.DMA
    pairs = [(9,), (4, 2, 8), (X,), (6,), (5, 8)]
    return pl.pallas_call(
        krylov_kernel,
        out_shape=(
            jax.ShapeDtypeStruct((256, 256), F32),
            jax.ShapeDtypeStruct((8, 8) + cell, F32),
        ),
        in_specs=[vmem(), vmem()],
        out_specs=(vmem(), vmem()),
        scratch_shapes=[
            pltpu.VMEM((8, 256, 256), BF16),
            pltpu.VMEM((1024, 256), F32),
            pltpu.VMEM((2, 8, 128, 128), BF16),
            pltpu.VMEM((2, 8, 128, 128), BF16),
            pltpu.VMEM((2, 8, 16, 128), F32),
            pltpu.VMEM((2, 8, 16, 128), F32),
            pltpu.VMEM((2, 16, 128), BF16),
            pltpu.VMEM((2, 8, 16, 128), BF16),
            pltpu.VMEM((2, 128, 128), BF16),
            pltpu.VMEM((2, 8, 128, 128), BF16),
            pltpu.VMEM((X, 256, 256), F32),
            pltpu.VMEM((X, 256, 256), F32),
            pltpu.VMEM((X, 256, 256), BF16),
            pltpu.VMEM((2, HALF, 256), BF16),
            pltpu.VMEM((2, 256, 256), BF16),
            pltpu.VMEM((8, 8) + cell, F32),
            pltpu.VMEM((8, 8) + cell, F32),
            pltpu.VMEM((8,) + cell, F32),
            pltpu.VMEM((8,) + cell, F32),
            pltpu.VMEM(cell, F32),
            pltpu.VMEM((8,) + cell, F32),
            pltpu.VMEM(cell, F32),
            pltpu.VMEM((8,) + cell, F32),
        ]
        + [dma(shape) for shape in pairs for _ in range(2)],
        compiler_params=pltpu.CompilerParams(
            collective_id=0, has_side_effects=True, vmem_limit_bytes=LIMIT
        ),
        name="krylov",
    )(own, tile)


PANEL = 32
N = 256


def factor_kernel(gram_ref, items_ref, basis_ref, factor_ref, a_ref, d_ref):
    for k in range(32):
        for c in range(2):
            a_ref[8 * k : 8 * k + 8, 128 * c : 128 * c + 128] = gram_ref[k // 4, (k % 4) * 2 + c]

    def panel(q, carry):
        base = q * PANEL
        rows = pl.ds(pl.multiple_of(base, PANEL), PANEL)
        w = pltpu.roll(a_ref[rows, :], lax.rem(N - base, N), 1)
        d = jnp.zeros((PANEL, 128), F32)
        for t in range(PANEL // 8):
            low = 8 * t
            part = w[low:, :]
            size = PANEL - low
            lane = lax.broadcasted_iota(jnp.int32, (size, N), 1)
            sub = lax.broadcasted_iota(jnp.int32, (size, N), 0) + low
            sub1 = sub[:, :128]
            columns = [
                jnp.broadcast_to(part[:, low + b : low + b + 1], (size, 128)) for b in range(8)
            ]
            d_part = d[low:, :]
            for a in range(8):
                r = low + a
                pivot = columns[a][a : a + 1, :]
                m = jnp.where(sub1 > r, columns[a] * (1.0 / pivot), 0.0)
                for b in range(a + 1, 8):
                    columns[b] = columns[b] - m * columns[b][a : a + 1, :]
                line = jnp.where(lane[:1] == r, 1.0, part[a : a + 1, :])
                kept = jnp.where((lane == r) & (sub > r), 0.0, part)
                part = kept - jnp.concatenate([m, m], axis=1) * line
                d_part = jnp.where(sub1 == r, pivot, d_part)
            w = part if low == 0 else jnp.concatenate([w[:low], part], axis=0)
            d = d_part if low == 0 else jnp.concatenate([d[:low], d_part], axis=0)
        d_ref[rows, :] = d
        lane = lax.broadcasted_iota(jnp.int32, (PANEL, N), 1)
        sub = lax.broadcasted_iota(jnp.int32, (PANEL, N), 0)
        d2 = jnp.concatenate([d, d], axis=1)
        ahead = (lane >= PANEL) & (lane < N - base)
        scaled = jnp.where(ahead, w / d2, 0.0)
        right = jnp.where((lane < PANEL) & (lane >= sub), jnp.where(lane == sub, 1.0, 0.0), w)
        a_ref[rows, :] = pltpu.roll(w, base, 1)
        scaled = pltpu.roll(scaled, base, 1)
        right = pltpu.roll(right, base, 1)
        update = lax.dot_general(
            scaled, right, (((0,), (0,)), ((), ())), precision=HIGH, preferred_element_type=F32
        )
        full_lane = lax.broadcasted_iota(jnp.int32, (N, N), 1)
        full_sub = lax.broadcasted_iota(jnp.int32, (N, N), 0)
        done = (full_sub >= base + PANEL) & (full_lane >= base) & (full_lane < base + PANEL)
        a_ref[...] = jnp.where(done, 0.0, a_ref[...]) - update
        return carry

    lax.fori_loop(0, N // PANEL, panel, 0)

    lane = lax.broadcasted_iota(jnp.int32, (N, N), 1)
    sub = lax.broadcasted_iota(jnp.int32, (N, N), 0)
    scale = 1.0 / jnp.sqrt(d_ref[...])
    scale = jnp.concatenate([scale, scale], axis=1)
    full = a_ref[...]
    factor_ref[...] = jnp.where(lane >= sub, full, 0.0) * scale
    inverse = jnp.where(lane < sub, full, jnp.where(lane == sub, 1.0, 0.0)) * scale
    basis_ref[...] = jnp.dot(
        inverse, items_ref[...], precision=HIGH, preferred_element_type=F32
    ).T


def factor_call(gram, items):
    return pl.pallas_call(
        factor_kernel,
        out_shape=(
            jax.ShapeDtypeStruct((256, 256), F32),
            jax.ShapeDtypeStruct((256, 256), F32),
        ),
        in_specs=[vmem(), vmem()],
        out_specs=(vmem(), vmem()),
        scratch_shapes=[pltpu.VMEM((N, N), F32), pltpu.VMEM((N, 128), F32)],
        compiler_params=pltpu.CompilerParams(vmem_limit_bytes=LIMIT),
        name="factor",
    )(gram, items)


def local(blocks, block_row, block_col, counts, start_block):
    tile = dense_tile(block_row[0, 0], block_col[0, 0], counts[0], blocks[0, 0])
    items, gram = krylov(start_block, tile)
    return factor_call(gram, items)


def solution(mesh):
    return jax.shard_map(
        local,
        mesh=mesh,
        in_specs=(
            P("rows", "cols", None, None, None),
            P("rows", "cols", None),
            P("rows", "cols", None),
            P("rows", "cols"),
            P(("cols", "rows"), None),
        ),
        out_specs=(P(("cols", "rows"), None), P()),
        check_vma=False,
    )
```

time: 921 us -> 113 us (0.12); the launches traced: 906 us -> 113 us
  other arithmetic: 266 us -> 0 us
  waiting for transfers between devices: 252 us -> 0 us
  blocking collectives: 235 us -> 0 us
  Pallas kernels: 0 us -> 107 us
  matrix products: 80.4 us -> 0 us
  between operations: 24.9 us -> 1.3 us
  local copies, waits for them, and re-layouts: 24.9 us -> 5.38 us
  starting transfers between devices: 19 us -> 0 us
    another operation x50 -> x0, other arithmetic: 262 us -> none  [the longest x42 208 us: local(): lower = jnp.linalg.cholesky(mine + theirs)]
    psum x1 -> x0, blocking collectives: 235 us -> none  [local(): user_tile = lax.psum(partial_value, 'cols').astype(jnp.bfloat16)]
    pallas_call x0 -> x3, Pallas kernels: none -> 107 us  [the longest x1 90 us: krylov(): pl.pallas_call(krylov_kernel, out_shape=(jax.ShapeDtypeStruct((256, 256),...]
    reduce_scatter x1 -> x0, waiting for transfers between devices: 83.1 us -> none  [local(): lax.psum_scatter(item_terms, 'rows', scatter_dimension=0, tiled=True)]
    dot_general x25 -> x0, matrix products: 76.1 us -> none  [the longest x3 24.8 us: backward_step(): jnp.einsum('ni,nbk->ibk', onehot, product, precision=lax.Precision.HIGHEST)]
    psum x1 -> x0, waiting for transfers between devices: 69.9 us -> none  [local(): lax.psum(gram_local.astype(jnp.bfloat16), 'rows').astype(jnp.float32)]
    ppermute x6 -> x0, waiting for transfers between devices: 62.1 us -> none  [swapped(): return lax.ppermute(block, axis, route)]
    all_gather x1 -> x0, waiting for transfers between devices: 36.3 us -> none  [local(): panel = lax.all_gather(start_block, 'rows', axis=0, tiled=True)]
  transfers between devices with their start and end apart: 9 -> 0, of which waited for: 9 -> 0; matrix products, arithmetic and copies ran while one was open for 0% -> 0% of each run, Pallas kernels for 0% -> 0%
where the time goes in v2:
time: 113 us
  Pallas kernels  107 us (95%)
  local copies, waits for them, and re-layouts  5.38 us (5%)
  between operations  1.3 us (1%)
    pallas_call x1, Pallas kernels, krylov(): pl.pallas_call(krylov_kernel, out_shape=(jax.ShapeDtypeStruct((256, 256),...  90 us
    pallas_call x1, Pallas kernels, factor_call(): pl.pallas_call(factor_kernel, out_shape=(jax.ShapeDtypeStruct((256, 256),...  12 us
    unnamed x10, local copies, waits for them, and re-layouts  5.38 us
    pallas_call x1, Pallas kernels, dense_tile(): pl.pallas_call(dense_kernel, grid=(NB // STEP,), out_shape=jax.ShapeDtype...  4.58 us

profile of v2, /device:TPU:1, one launch (start us, length us, event | category | flops | bytes accessed | tf_op | source)
XLA Modules:
  0.0 113.2 jit_solution(15516243753376927530)
XLA Ops:
  1.3 0.0 copy-start.1
  1.3 1.9 %copy-done.1 = bf16[1,1,96,128,128]{4,3,2,1,0:T(8,128)(2,1)S(1)} copy-done((bf16[1,1,96,128,128]{4,3,2,1,0:T(8,128)(2,1)S(1)}, bf16[1,1,96,128,128]{4,3,2,1,0:T(8,128)(2,1)}, u32[]{:S(2)}) %copy-start.1) | copy-done | bytes 3145752
  3.2 0.0 copy-start.3
  3.2 0.7 copy-done.3
  3.8 0.0 copy-start.4
  3.8 0.7 copy-done.4
  4.5 0.0 copy-start.2
  4.5 4.6 %dense_tile.1.tile_ref = bf16[8,1024,256]{2,1,0:T(8,128)(2,1)} custom-call(s32[96]{0:T(128)S(1)} %bitcast.6, s32[96]{0:T(128)S(1)} %bitcast.7, s32[1]{0:T(128)} %bitcast.4.count_ref, bf16[96,128,128]{2,1,0:T(8,128)(2,1)S(1)} %bitcast.5), custom_call_target="tpu_custom_call" | custom-call | tf_op jit(solution)/shard_map/dense_tile/pallas_call | solution.py:99
  9.1 0.0 copy-done.2
  9.1 0.0 copy-start
  9.1 2.2 %copy-done = bf16[8,1024,256]{2,1,0:T(8,128)(2,1)S(1)} copy-done((bf16[8,1024,256]{2,1,0:T(8,128)(2,1)S(1)}, bf16[8,1024,256]{2,1,0:T(8,128)(2,1)}, u32[]{:S(2)}) %copy-start) | copy-done | bytes 4194328
  11.3 90.0 %krylov.1 = (f32[256,256]{1,0:T(8,128)S(1)}, f32[8,8,8,128]{3,2,1,0:T(8,128)S(1)}) custom-call(bf16[256,256]{1,0:T(8,128)(2,1)S(1)} %copy-done.2, bf16[8,1024,256]{2,1,0:T(8,128)(2,1)S(1)} %copy-done), custom_call_target="tpu_custom_call" | custom-call | tf_op jit(solution)/shard_map/krylov/pallas_call | solution.py:350
  101.3 12.0 %factor.1 = (f32[256,256]{1,0:T(8,128)}, f32[256,256]{1,0:T(8,128)}) custom-call(f32[8,8,8,128]{3,2,1,0:T(8,128)S(1)} %get-tuple-element.4.gram_ref, f32[256,256]{1,0:T(8,128)S(1)} %get-tuple-element.5.items_ref), custom_call_target="tpu_custom_call" | custom-call | tf_op jit(solution)/shard_map/factor/pallas_call | solution.py:462
Async XLA Ops:
  1.3 1.9 %copy-start.1 = (bf16[1,1,96,128,128]{4,3,2,1,0:T(8,128)(2,1)S(1)}, bf16[1,1,96,128,128]{4,3,2,1,0:T(8,128)(2,1)}, u32[]{:S(2)}) copy-start(bf16[1,1,96,128,128]{4,3,2,1,0:T(8,128)(2,1)} %param.5) | copy-start | bytes 9437188
  3.2 0.7 copy-start.3
  3.8 0.7 copy-start.4
  4.5 4.6 %copy-start.2 = (bf16[256,256]{1,0:T(8,128)(2,1)S(1)}, bf16[256,256]{1,0:T(8,128)(2,1)}, u32[]{:S(2)}) copy-start(bf16[256,256]{1,0:T(8,128)(2,1)} %own_ref.1) | copy-start | bytes 393220
  9.1 2.2 %copy-start = (bf16[8,1024,256]{2,1,0:T(8,128)(2,1)S(1)}, bf16[8,1024,256]{2,1,0:T(8,128)(2,1)}, u32[]{:S(2)}) copy-start(bf16[8,1024,256]{2,1,0:T(8,128)(2,1)} %dense_tile.1.tile_ref) | copy-start | bytes 12582916

commit v3 on v2

v3 whole, which is shorter than its diff:
```python
import jax
import jax.numpy as jnp
from jax import lax
from jax.experimental import pallas as pl
from jax.experimental.pallas import tpu as pltpu
from jax.sharding import PartitionSpec as P

MESH = pl.DeviceIdType.MESH
F32 = jnp.float32
BF16 = jnp.bfloat16
HIGH = lax.Precision.HIGHEST
LIMIT = 63 * 1024 * 1024
NB = 96
GROUP = 8
STEP = 24
X, Y, Z = 4, 8, 8


def vmem():
    return pl.BlockSpec(memory_space=pltpu.VMEM)


def smem():
    return pl.BlockSpec(memory_space=pltpu.SMEM)


def remote(src, dst, send, recv, device):
    return pltpu.make_async_remote_copy(
        src_ref=src, dst_ref=dst, send_sem=send, recv_sem=recv, device_id=device, device_id_type=MESH
    )


def places():
    row = lax.axis_index("rows")
    col = lax.axis_index("cols")
    return row, col, lax.div(col, Z), lax.rem(col, Z)


def each(count, body):
    def step(i, carry):
        body(i)
        return carry

    lax.fori_loop(1, count, step, 0)


def ring(me, i, count):
    return lax.rem(me + i, count)


def greet(makers):
    barrier = pltpu.get_barrier_semaphore()
    total = 0
    for count, device in makers:
        each(
            count,
            lambda i, device=device: pl.semaphore_signal(
                barrier, inc=1, device_id=device(i), device_id_type=MESH
            ),
        )
        total += count - 1
    pl.semaphore_wait(barrier, total)


def dense_kernel(rows_ref, cols_ref, count_ref, tiles_ref, out_ref, acc_ref, pack_ref, sem):
    step = pl.program_id(0)

    @pl.when(step == 0)
    def _():
        acc_ref[...] = jnp.zeros_like(acc_ref)

    count = count_ref[0]

    def group(g, carry):
        for j in range(GROUP):
            at = g * GROUP + j
            slot = step * STEP + at
            tile = jnp.where(slot < count, tiles_ref[at].astype(F32), 0.0)
            place = cols_ref[slot]
            acc_ref[lax.div(place, 2), lax.rem(place, 2), rows_ref[slot]] += tile
        return carry

    lax.fori_loop(0, STEP // GROUP, group, 0)

    @pl.when(step == NB // STEP - 1)
    def _():
        def out_copy(q):
            return pltpu.make_async_copy(pack_ref.at[q], out_ref.at[q], sem.at[q])

        def chunk(q, carry):
            for u in range(8):
                for e in range(2):
                    pack_ref[q, u * 128 : (u + 1) * 128, e * 128 : (e + 1) * 128] = acc_ref[
                        q, e, u
                    ].astype(BF16)
            out_copy(q).start()
            return carry

        def finish(q, carry):
            out_copy(q).wait()
            return carry

        lax.fori_loop(0, 8, chunk, 0)
        lax.fori_loop(0, 8, finish, 0)


def dense_tile(rows, cols, count, tiles):
    return pl.pallas_call(
        dense_kernel,
        grid=(NB // STEP,),
        out_shape=jax.ShapeDtypeStruct((8, 1024, 256), BF16),
        in_specs=[smem(), smem(), smem(), pl.BlockSpec((STEP, 128, 128), lambda i: (i, 0, 0))],
        out_specs=pl.BlockSpec(memory_space=pl.ANY),
        scratch_shapes=[
            pltpu.VMEM((8, 2, 8, 128, 128), F32),
            pltpu.VMEM((8, 1024, 256), BF16),
            pltpu.SemaphoreType.DMA((8,)),
        ],
        compiler_params=pltpu.CompilerParams(
            dimension_semantics=("arbitrary",), vmem_limit_bytes=LIMIT
        ),
        name="dense_tile",
    )(rows, cols, count, tiles)


HALF = 128
FAR_FIRST = (4, 3, 5, 2, 6, 1, 7)


def krylov_kernel(
    own_ref, dense_ref, items_ref, gram_ref,
    tile, panel, acc, part, got1, sum1, got2, mine, wide, turned, users,
    give, near, pack, relay, far, cut, gram1, gsum1, gram2, gsum2, gram3, gsum3, gwide,
    load, send_p, recv_p, send_u, recv_u, send_a, recv_a, send_b, recv_b, send_g, recv_g,
):
    row, col, y, z = places()
    chip, core = lax.div(row, 2), lax.rem(row, 2)
    other = 1 - core
    partner = (chip * 2 + other, col)
    spots = {"r": row, "y": y, "z": z}
    low, high = pl.ds(0, HALF), pl.ds(HALF, HALF)

    def spot(i, which):
        return ring(chip, i, X) * 2 + which

    def beside(i):
        return (spot(i, core), col)

    def along(axis, i):
        target = ring(spots[axis], i, 8)
        if axis == "r":
            return target, (target, col)
        if axis == "y":
            return target, (row, target * Z + z)
        return target, (row, y * Z + target)

    order = [(i, which) for i in (0, 3, 1, 2) for which in (core, other)]
    fetches = [
        pltpu.make_async_copy(dense_ref.at[spot(*at)], tile.at[spot(*at)], load.at[n])
        for n, at in enumerate(order)
    ]
    mine_copy = pltpu.make_async_copy(own_ref, panel.at[row], load.at[8])
    mine_copy.start()
    for fetch in fetches:
        fetch.start()

    greet([(8, lambda i, axis=axis: along(axis, i)[1]) for axis in "ryz"])

    pending = []

    def push(src, dst, sends, recvs, n, device):
        copy = remote(src, dst, sends.at[n], recvs.at[n], device)
        copy.start()
        pending.append(copy)

    def landed(dst, sends, recvs, n):
        remote(dst, dst, sends.at[n], recvs.at[n], partner).wait_recv()

    def drain(keep=0):
        while len(pending) > keep:
            pending.pop(0).wait_send()

    p = (send_p, recv_p)
    done = []

    def product(i, which):
        n = len(done)
        done.append(n)
        fetches[n].wait()
        q = spot(*order[n])
        return jnp.dot(tile[q], panel[q], preferred_element_type=F32)

    push(own_ref, panel.at[row], *p, 1, beside(1))
    push(own_ref, panel.at[row], *p, 2, beside(3))
    push(own_ref, panel.at[row], *p, 0, partner)
    mine_copy.wait()
    acc[...] = product(0, core)
    landed(panel.at[spot(0, other)], *p, 0)
    acc[...] += product(0, other)
    prev, nxt, over = spot(3, core), spot(1, core), spot(2, core)
    landed(panel.at[prev], *p, 1)
    push(panel.at[prev, low], panel.at[prev, low], *p, 3, beside(1))
    landed(panel.at[nxt], *p, 2)
    push(panel.at[nxt, high], panel.at[nxt, high], *p, 4, beside(3))
    push(panel.at[prev], panel.at[prev], *p, 5, partner)
    push(panel.at[nxt], panel.at[nxt], *p, 6, partner)
    acc[...] += product(3, core)
    landed(panel.at[spot(3, other)], *p, 5)
    acc[...] += product(3, other)
    landed(panel.at[over, low], *p, 3)
    push(panel.at[over, low], panel.at[over, low], *p, 7, partner)
    landed(panel.at[over, high], *p, 4)
    push(panel.at[over, high], panel.at[over, high], *p, 8, partner)
    acc[...] += product(1, core)
    landed(panel.at[spot(1, other)], *p, 6)
    acc[...] += product(1, other)
    acc[...] += product(2, core)
    last = spot(2, other)
    landed(panel.at[last, low], *p, 7)
    landed(panel.at[last, high], *p, 8)
    total = acc[...] + product(2, other)
    for u in range(8):
        for h in range(2):
            part[h, u] = total[u * 128 : (u + 1) * 128, h * 128 : (h + 1) * 128].astype(BF16)

    def scatter(axis, source, landing, sends, recvs, i):
        target, device = along(axis, i)
        push(source(target), landing.at[spots[axis]], sends, recvs, i, device)

    def gathered(axis, landing, sends, recvs):
        for i in FAR_FIRST[::-1]:
            landed(landing.at[ring(spots[axis], 8 - i, 8)], sends, recvs, i)

    def u(stage, h):
        return send_u.at[stage, h], recv_u.at[stage, h]

    me, first, second = (y, z), ("y", "z"), ("z", "y")
    for i in FAR_FIRST:
        for h in range(2):
            scatter(first[h], lambda t, h=h: part.at[h, t], got1.at[h], *u(0, h), i)
    for h in range(2):
        got1[h, me[h]] = part[h, me[h]]
    drain(14)
    for h in range(2):
        gathered(first[h], got1.at[h], *u(0, h))
        total = got1[h, 0].astype(F32)
        for k in range(1, 8):
            total = total + got1[h, k].astype(F32)
        sum1[h] = total.reshape(8, 16, 128)
        for i in FAR_FIRST:
            scatter(second[h], lambda t, h=h: sum1.at[h, t], got2.at[h], *u(1, h), i)
        got2[h, me[1 - h]] = sum1[h, me[1 - h]]
    drain(14)
    for h in range(2):
        gathered(second[h], got2.at[h], *u(1, h))
        total = got2[h, 0]
        for k in range(1, 8):
            total = total + got2[h, k]
        mine[h] = total.astype(BF16)
        for i in FAR_FIRST:
            scatter(second[h], lambda t, h=h: mine.at[h], wide.at[h], *u(2, h), i)
        wide[h, me[1 - h]] = mine[h]
    drain(14)

    def up(h, d, src, dst):
        push(src, dst, *u(3, h), d - 1, along(first[h], 1)[1])

    def down(h, d, src, dst):
        push(src, dst, *u(3, h), d + 3, along(first[h], 7)[1])

    for h in range(2):
        gathered(second[h], wide.at[h], *u(2, h))
        turned[h] = wide[h].reshape(128, 128).astype(F32).T.astype(BF16)
        up(h, 1, turned.at[h], users.at[h, me[h]])
        down(h, 1, turned.at[h], users.at[h, me[h]])
        users[h, me[h]] = turned[h]
    drain(4)
    upper, lower = pl.ds(0, 64), pl.ds(64, 64)
    for d in range(1, 4):
        for h in range(2):
            below = users.at[h, ring(me[h], 8 - d, 8)]
            landed(below, *u(3, h), d - 1)
            if d == 3:
                below = below.at[upper]
            up(h, d + 1, below, below)
            above = users.at[h, ring(me[h], d, 8)]
            landed(above, *u(3, h), d + 3)
            if d == 3:
                above = above.at[lower]
            down(h, d + 1, above, above)
    for h in range(2):
        across = users.at[h, ring(me[h], 4, 8)]
        landed(across.at[upper], *u(3, h), 3)
        landed(across.at[lower], *u(3, h), 7)

    def term(i, which):
        left = jnp.concatenate(
            [jnp.concatenate([users[h, k] for k in range(8)], axis=1) for h in range(2)], axis=0
        )
        return jnp.dot(left, tile[spot(i, which)], preferred_element_type=F32)

    a, b = (send_a, recv_a), (send_b, recv_b)

    def lend(i):
        give[i] = term(i, other)
        push(give.at[i], near.at[i], *a, i, partner)

    lend(2)
    lend(1)
    value = term(2, core)
    landed(near.at[2], *a, 2)
    pack[2] = (value + near[2]).astype(BF16)
    push(pack.at[2, low], relay.at[0], *b, 0, beside(1))
    push(pack.at[2, high], relay.at[1], *b, 1, beside(3))
    lend(3)
    value = term(1, core)
    landed(near.at[1], *a, 1)
    near[1] = value + near[1]
    pack[1, HALF:] = near[1, HALF:].astype(BF16)
    push(pack.at[1, high], far.at[0, high], *b, 2, beside(1))
    lend(0)
    value = term(3, core)
    landed(near.at[3], *a, 3)
    near[3] = value + near[3]
    pack[3, :HALF] = near[3, :HALF].astype(BF16)
    push(pack.at[3, low], far.at[1, low], *b, 3, beside(3))
    landed(relay.at[0], *b, 0)
    pack[1, :HALF] = (near[1, :HALF] + relay[0].astype(F32)).astype(BF16)
    push(pack.at[1, low], far.at[0, low], *b, 4, beside(1))
    landed(relay.at[1], *b, 1)
    pack[3, HALF:] = (near[3, HALF:] + relay[1].astype(F32)).astype(BF16)
    push(pack.at[3, high], far.at[1, high], *b, 5, beside(3))
    value = term(0, core)
    landed(near.at[0], *a, 0)
    near[0] = value + near[0]
    drain(2)
    landed(far.at[0, high], *b, 2)
    landed(far.at[1, low], *b, 3)
    landed(far.at[0, low], *b, 4)
    landed(far.at[1, high], *b, 5)
    items = near[0] + far[0].astype(F32) + far[1].astype(F32)
    items_ref[...] = items

    gram = lax.dot_general(
        items, items, (((1,), (1,)), ((), ())), precision=HIGH, preferred_element_type=F32
    )
    for k in range(16):
        for c in range(2):
            cut[k // 2, (k % 2) * 2 + c] = gram[
                16 * k : 16 * k + 16, 128 * c : 128 * c + 128
            ].astype(BF16)

    def g(n):
        return send_g.at[n], recv_g.at[n]

    def move(n, axis, source, landing):
        for i in FAR_FIRST:
            scatter(axis, source, landing, *g(n), i)
        landing[spots[axis]] = source(spots[axis])[...]
        drain(7)
        gathered(axis, landing, *g(n))

    def summed(got):
        total = got[0]
        for k in range(1, 8):
            total = total + got[k]
        return total

    move(0, "r", lambda t: cut.at[t], gram1)
    total = gram1[0].astype(F32)
    for k in range(1, 8):
        total = total + gram1[k].astype(F32)
    gsum1[...] = total.reshape(8, 8, 128)
    move(1, "y", lambda t: gsum1.at[t], gram2)
    gsum2[...] = summed(gram2)
    move(2, "z", lambda t: gsum2, gram3)
    gsum3[...] = summed(gram3)
    move(3, "y", lambda t: gsum3, gwide)
    for i in (2, 1, 3):
        push(gwide, gram_ref.at[row], *g(4), i, beside(i))
    push(gwide, gram_ref.at[row], *g(4), 0, partner)
    gram_ref[row] = gwide[...]
    drain(4)
    for i in (3, 1, 2):
        block = gram_ref.at[spot(4 - i, core)]
        landed(block, *g(4), i)
        push(block, block, *g(4), 4 + i, partner)
    landed(gram_ref.at[spot(0, other)], *g(4), 0)
    for i in (3, 1, 2):
        landed(gram_ref.at[spot(4 - i, other)], *g(4), 4 + i)
    drain()


def krylov(own, tile):
    cell = (8, 128)
    dma = pltpu.SemaphoreType.DMA
    pairs = [(9,), (4, 2, 8), (X,), (6,), (5, 8)]
    return pl.pallas_call(
        krylov_kernel,
        out_shape=(
            jax.ShapeDtypeStruct((256, 256), F32),
            jax.ShapeDtypeStruct((8, 8) + cell, F32),
        ),
        in_specs=[pl.BlockSpec(memory_space=pl.ANY), pl.BlockSpec(memory_space=pl.ANY)],
        out_specs=(vmem(), vmem()),
        scratch_shapes=[
            pltpu.VMEM((8, 1024, 256), BF16),
            pltpu.VMEM((8, 256, 256), BF16),
            pltpu.VMEM((1024, 256), F32),
            pltpu.VMEM((2, 8, 128, 128), BF16),
            pltpu.VMEM((2, 8, 128, 128), BF16),
            pltpu.VMEM((2, 8, 16, 128), F32),
            pltpu.VMEM((2, 8, 16, 128), F32),
            pltpu.VMEM((2, 16, 128), BF16),
            pltpu.VMEM((2, 8, 16, 128), BF16),
            pltpu.VMEM((2, 128, 128), BF16),
            pltpu.VMEM((2, 8, 128, 128), BF16),
            pltpu.VMEM((X, 256, 256), F32),
            pltpu.VMEM((X, 256, 256), F32),
            pltpu.VMEM((X, 256, 256), BF16),
            pltpu.VMEM((2, HALF, 256), BF16),
            pltpu.VMEM((2, 256, 256), BF16),
            pltpu.VMEM((8, 4, 16, 128), BF16),
            pltpu.VMEM((8, 4, 16, 128), BF16),
            pltpu.VMEM((8,) + cell, F32),
            pltpu.VMEM((8,) + cell, F32),
            pltpu.VMEM(cell, F32),
            pltpu.VMEM((8,) + cell, F32),
            pltpu.VMEM(cell, F32),
            pltpu.VMEM((8,) + cell, F32),
            dma((9,)),
        ]
        + [dma(shape) for shape in pairs for _ in range(2)],
        compiler_params=pltpu.CompilerParams(
            collective_id=0, has_side_effects=True, vmem_limit_bytes=LIMIT
        ),
        name="krylov",
    )(own, tile)


PANEL = 32
N = 256


def factor_kernel(gram_ref, items_ref, basis_ref, factor_ref, a_ref, d_ref):
    for k in range(32):
        for c in range(2):
            a_ref[8 * k : 8 * k + 8, 128 * c : 128 * c + 128] = gram_ref[
                k // 4, (k // 2 % 2) * 4 + c * 2 + k % 2
            ]

    def panel(q, carry):
        base = q * PANEL
        rows = pl.ds(pl.multiple_of(base, PANEL), PANEL)
        w = pltpu.roll(a_ref[rows, :], lax.rem(N - base, N), 1)
        d = jnp.zeros((PANEL, 128), F32)
        for t in range(PANEL // 8):
            low = 8 * t
            part = w[low:, :]
            size = PANEL - low
            lane = lax.broadcasted_iota(jnp.int32, (size, N), 1)
            sub = lax.broadcasted_iota(jnp.int32, (size, N), 0) + low
            sub1 = sub[:, :128]
            columns = [
                jnp.broadcast_to(part[:, low + b : low + b + 1], (size, 128)) for b in range(8)
            ]
            d_part = d[low:, :]
            for a in range(0, 8, 2):
                r = low + a
                one, two = columns[a], columns[a + 1]
                p11, p12 = one[a : a + 1, :], two[a : a + 1, :]
                p21, p22 = one[a + 1 : a + 2, :], two[a + 1 : a + 2, :]
                inv1 = 1.0 / p11
                inv2 = p11 * (1.0 / (p11 * p22 - p21 * p12))
                ratio = p21 * inv1
                m1 = jnp.where(sub1 > r, one * inv1, 0.0)
                m2 = jnp.where(sub1 > r + 1, (two - m1 * p12) * inv2, 0.0)
                for b in range(a + 2, 8):
                    top = columns[b][a : a + 1, :]
                    next_top = columns[b][a + 1 : a + 2, :] - ratio * top
                    columns[b] = columns[b] - m1 * top - m2 * next_top
                lane1 = lane[:1]
                line1 = jnp.where(lane1 == r, 1.0, part[a : a + 1, :])
                ratio2 = jnp.concatenate([ratio, ratio], axis=1)
                line2 = jnp.where(lane1 == r, 0.0, part[a + 1 : a + 2, :]) - ratio2 * line1
                line1 = jnp.where(lane1 == r + 1, 0.0, line1)
                line2 = jnp.where(lane1 == r + 1, 1.0, line2)
                gone = ((lane == r) & (sub > r)) | ((lane == r + 1) & (sub > r + 1))
                part = (
                    jnp.where(gone, 0.0, part)
                    - jnp.concatenate([m1, m1], axis=1) * line1
                    - jnp.concatenate([m2, m2], axis=1) * line2
                )
                d_part = jnp.where(sub1 == r, p11, d_part)
                d_part = jnp.where(sub1 == r + 1, p22 - ratio * p12, d_part)
            w = part if low == 0 else jnp.concatenate([w[:low], part], axis=0)
            d = d_part if low == 0 else jnp.concatenate([d[:low], d_part], axis=0)
        d_ref[rows, :] = d
        lane = lax.broadcasted_iota(jnp.int32, (PANEL, N), 1)
        sub = lax.broadcasted_iota(jnp.int32, (PANEL, N), 0)
        d2 = jnp.concatenate([d, d], axis=1)
        ahead = (lane >= PANEL) & (lane < N - base)
        scaled = jnp.where(ahead, w / d2, 0.0)
        right = jnp.where((lane < PANEL) & (lane >= sub), jnp.where(lane == sub, 1.0, 0.0), w)
        a_ref[rows, :] = pltpu.roll(w, base, 1)
        scaled = pltpu.roll(scaled, base, 1)
        right = pltpu.roll(right, base, 1)
        update = lax.dot_general(
            scaled, right, (((0,), (0,)), ((), ())), precision=HIGH, preferred_element_type=F32
        )
        full_lane = lax.broadcasted_iota(jnp.int32, (N, N), 1)
        full_sub = lax.broadcasted_iota(jnp.int32, (N, N), 0)
        done = (full_sub >= base + PANEL) & (full_lane >= base) & (full_lane < base + PANEL)
        a_ref[...] = jnp.where(done, 0.0, a_ref[...]) - update
        return carry

    lax.fori_loop(0, N // PANEL, panel, 0)

    lane = lax.broadcasted_iota(jnp.int32, (N, N), 1)
    sub = lax.broadcasted_iota(jnp.int32, (N, N), 0)
    pivots = d_ref[...]
    scale = 1.0 / jnp.sqrt(pivots)
    scale = jnp.concatenate([scale, scale], axis=1)
    full = jnp.where(lane == sub, jnp.concatenate([pivots, pivots], axis=1), a_ref[...])
    factor_ref[...] = jnp.where(lane >= sub, full, 0.0) * scale
    inverse = jnp.where(lane < sub, full, jnp.where(lane == sub, 1.0, 0.0)) * scale
    basis_ref[...] = jnp.dot(
        inverse, items_ref[...], precision=HIGH, preferred_element_type=F32
    ).T


def factor_call(gram, items):
    return pl.pallas_call(
        factor_kernel,
        out_shape=(
            jax.ShapeDtypeStruct((256, 256), F32),
            jax.ShapeDtypeStruct((256, 256), F32),
        ),
        in_specs=[vmem(), vmem()],
        out_specs=(vmem(), vmem()),
        scratch_shapes=[pltpu.VMEM((N, N), F32), pltpu.VMEM((N, 128), F32)],
        compiler_params=pltpu.CompilerParams(vmem_limit_bytes=LIMIT),
        name="factor",
    )(gram, items)


def local(blocks, block_row, block_col, counts, start_block):
    tile = dense_tile(block_row[0, 0], block_col[0, 0], counts[0], blocks[0, 0])
    items, gram = krylov(start_block, tile)
    return factor_call(gram, items)


def solution(mesh):
    return jax.shard_map(
        local,
        mesh=mesh,
        in_specs=(
            P("rows", "cols", None, None, None),
            P("rows", "cols", None),
            P("rows", "cols", None),
            P("rows", "cols"),
            P(("cols", "rows"), None),
        ),
        out_specs=(P(("cols", "rows"), None), P()),
        check_vma=False,
    )
```

time: 113 us -> 113 us (level)
  local copies, waits for them, and re-layouts: 5.38 us -> 0 us
  Pallas kernels: 107 us -> 112 us
    unnamed x10 -> x0, local copies, waits for them, and re-layouts: 5.38 us -> none
    pallas_call x1, Pallas kernels: 90 us -> 93.3 us  [krylov(): pl.pallas_call(krylov_kernel, out_shape=(jax.ShapeDtypeStruct((256, 256),...]
    pallas_call x1, Pallas kernels: 4.58 us -> 5.73 us  [dense_tile(): pl.pallas_call(dense_kernel, grid=(NB // STEP,), out_shape=jax.ShapeDtype...]
where the time goes in v3:
time: 113 us
  Pallas kernels  112 us (99%)
  between operations  1.29 us (1%)
    pallas_call x1, Pallas kernels, krylov(): pl.pallas_call(krylov_kernel, out_shape=(jax.ShapeDtypeStruct((256, 256),...  93.3 us
    pallas_call x1, Pallas kernels, factor_call(): pl.pallas_call(factor_kernel, out_shape=(jax.ShapeDtypeStruct((256, 256),...  12.6 us
    pallas_call x1, Pallas kernels, dense_tile(): pl.pallas_call(dense_kernel, grid=(NB // STEP,), out_shape=jax.ShapeDtype...  5.73 us

profile of v3, /device:TPU:1, one launch (start us, length us, event | category | flops | bytes accessed | tf_op | source)
XLA Modules:
  0.0 113.0 jit_solution(10915141044020684244)
XLA Ops:
  1.3 5.7 %dense_tile.1.dense_ref = bf16[8,1024,256]{2,1,0:T(8,128)(2,1)} custom-call(s32[96]{0:T(128)} %bitcast.6, s32[96]{0:T(128)} %bitcast.7, s32[1]{0:T(128)} %bitcast.4.count_ref, bf16[96,128,128]{2,1,0:T(8,128)(2,1)} %bitcast.5), custom_call_target="tpu_custom_call" | custom-call | tf_op jit(solution)/shard_map/dense_tile/pallas_call | solution.py:108
  7.0 93.3 %krylov.1 = (f32[256,256]{1,0:T(8,128)}, f32[8,8,8,128]{3,2,1,0:T(8,128)}) custom-call(bf16[256,256]{1,0:T(8,128)(2,1)} %own_ref.1, bf16[8,1024,256]{2,1,0:T(8,128)(2,1)} %dense_tile.1.dense_ref), custom_call_target="tpu_custom_call" | custom-call | tf_op jit(solution)/shard_map/krylov/pallas_call | solution.py:398
  100.4 12.6 %factor.1 = (f32[256,256]{1,0:T(8,128)}, f32[256,256]{1,0:T(8,128)}) custom-call(f32[8,8,8,128]{3,2,1,0:T(8,128)} %get-tuple-element.4.gram_ref, f32[256,256]{1,0:T(8,128)} %get-tuple-element.5.items_ref), custom_call_target="tpu_custom_call" | custom-call | tf_op jit(solution)/shard_map/factor/pallas_call | solution.py:533

commit v4 on v3

--- a/solution.py
+++ b/solution.py
@@ -10,6 +10,7 @@
 BF16 = jnp.bfloat16
 HIGH = lax.Precision.HIGHEST
 LIMIT = 63 * 1024 * 1024
+ROOM = 53 * 1024 * 1024
 NB = 96
 GROUP = 8
 STEP = 24
@@ -72,12 +73,20 @@
     count = count_ref[0]
 
     def group(g, carry):
-        for j in range(GROUP):
-            at = g * GROUP + j
-            slot = step * STEP + at
-            tile = jnp.where(slot < count, tiles_ref[at].astype(F32), 0.0)
-            place = cols_ref[slot]
-            acc_ref[lax.div(place, 2), lax.rem(place, 2), rows_ref[slot]] += tile
+        for j in range(0, GROUP, 2):
+            spots, tiles = [], []
+            for k in range(2):
+                at = g * GROUP + j + k
+                slot = step * STEP + at
+                col = cols_ref[slot]
+                spots.append((lax.div(col, 2), lax.rem(col, 2), rows_ref[slot]))
+                tiles.append(jnp.where(slot < count, tiles_ref[at].astype(F32), 0.0))
+            same = (spots[0][0] == spots[1][0]) & (spots[0][1] == spots[1][1])
+            same = same & (spots[0][2] == spots[1][2])
+            one = acc_ref[spots[0]] + tiles[0]
+            two = jnp.where(same, one, acc_ref[spots[1]]) + tiles[1]
+            acc_ref[spots[0]] = one
+            acc_ref[spots[1]] = two
         return carry
 
     lax.fori_loop(0, STEP // GROUP, group, 0)
@@ -88,11 +97,13 @@
             return pltpu.make_async_copy(pack_ref.at[q], out_ref.at[q], sem.at[q])
 
         def chunk(q, carry):
-            for u in range(8):
+            def block(u, inner):
+                rows = pl.ds(pl.multiple_of(u * 128, 128), 128)
                 for e in range(2):
-                    pack_ref[q, u * 128 : (u + 1) * 128, e * 128 : (e + 1) * 128] = acc_ref[
-                        q, e, u
-                    ].astype(BF16)
+                    pack_ref[q, rows, e * 128 : (e + 1) * 128] = acc_ref[q, e, u].astype(BF16)
+                return inner
+
+            lax.fori_loop(0, 8, block, 0)
             out_copy(q).start()
             return carry
 
@@ -124,13 +135,18 @@
 
 
 HALF = 128
-FAR_FIRST = (4, 3, 5, 2, 6, 1, 7)
+def table(digits):
+    return sum(digit * 8**n for n, digit in enumerate(digits))
+
+
+FORWARD = (0, 1, 6, 7, 2, 3, 4, 5)
+BACKWARD = (5, 3, 4, 7, 2, 1, 6, 0)
 
 
 def krylov_kernel(
     own_ref, dense_ref, items_ref, gram_ref,
     tile, panel, acc, part, got1, sum1, got2, mine, wide, turned, users,
-    give, near, pack, relay, far, cut, gram1, gsum1, gram2, gsum2, gram3, gsum3, gwide,
+    value, near, pack, relay, far, cut, gram1, gsum1, gram2, gsum2, gram3, gsum3, gwide,
     load, send_p, recv_p, send_u, recv_u, send_a, recv_a, send_b, recv_b, send_g, recv_g,
 ):
     row, col, y, z = places()
@@ -143,6 +159,9 @@
     def spot(i, which):
         return ring(chip, i, X) * 2 + which
 
+    def place(digit):
+        return spot(lax.div(digit, 2), lax.rem(core + lax.rem(digit, 2), 2))
+
     def beside(i):
         return (spot(i, core), col)
 
@@ -154,186 +173,236 @@
             return target, (row, target * Z + z)
         return target, (row, y * Z + target)
 
-    order = [(i, which) for i in (0, 3, 1, 2) for which in (core, other)]
-    fetches = [
-        pltpu.make_async_copy(dense_ref.at[spot(*at)], tile.at[spot(*at)], load.at[n])
-        for n, at in enumerate(order)
-    ]
+    def fetch(digit):
+        q = place(digit)
+        return pltpu.make_async_copy(dense_ref.at[q], tile.at[q], load.at[digit])
+
+    def fetch_next(n, digits):
+        fetch(lax.rem(digits, 8)).start()
+        return lax.div(digits, 8)
+
     mine_copy = pltpu.make_async_copy(own_ref, panel.at[row], load.at[8])
     mine_copy.start()
-    for fetch in fetches:
-        fetch.start()
+    lax.fori_loop(0, 8, fetch_next, table(FORWARD))
 
     greet([(8, lambda i, axis=axis: along(axis, i)[1]) for axis in "ryz"])
-
-    pending = []
-
-    def push(src, dst, sends, recvs, n, device):
-        copy = remote(src, dst, sends.at[n], recvs.at[n], device)
-        copy.start()
-        pending.append(copy)
 
     def landed(dst, sends, recvs, n):
         remote(dst, dst, sends.at[n], recvs.at[n], partner).wait_recv()
 
-    def drain(keep=0):
-        while len(pending) > keep:
-            pending.pop(0).wait_send()
-
+    def far_first(body):
+        def step(n, carry):
+            body(4 + lax.div(n + 1, 2) * (1 - 2 * lax.rem(n, 2)))
+            return carry
+
+        lax.fori_loop(0, 7, step, 0)
+
+    prev, nxt, over = spot(3, core), spot(1, core), spot(2, core)
+    last = spot(2, other)
     p = (send_p, recv_p)
-    done = []
-
-    def product(i, which):
-        n = len(done)
-        done.append(n)
-        fetches[n].wait()
-        q = spot(*order[n])
-        return jnp.dot(tile[q], panel[q], preferred_element_type=F32)
-
-    push(own_ref, panel.at[row], *p, 1, beside(1))
-    push(own_ref, panel.at[row], *p, 2, beside(3))
-    push(own_ref, panel.at[row], *p, 0, partner)
+    hops = [
+        (own_ref, panel.at[row], partner),
+        (own_ref, panel.at[row], beside(1)),
+        (own_ref, panel.at[row], beside(3)),
+        (panel.at[prev, low], panel.at[prev, low], beside(1)),
+        (panel.at[nxt, high], panel.at[nxt, high], beside(3)),
+        (panel.at[prev], panel.at[prev], partner),
+        (panel.at[nxt], panel.at[nxt], partner),
+        (panel.at[over, low], panel.at[over, low], partner),
+        (panel.at[over, high], panel.at[over, high], partner),
+    ]
+
+    def hop(n):
+        src, dst, device = hops[n]
+        return remote(src, dst, send_p.at[n], recv_p.at[n], device)
+
+    for n in (1, 2, 0):
+        hop(n).start()
+    acc[...] = jnp.zeros_like(acc)
     mine_copy.wait()
-    acc[...] = product(0, core)
-    landed(panel.at[spot(0, other)], *p, 0)
-    acc[...] += product(0, other)
-    prev, nxt, over = spot(3, core), spot(1, core), spot(2, core)
-    landed(panel.at[prev], *p, 1)
-    push(panel.at[prev, low], panel.at[prev, low], *p, 3, beside(1))
-    landed(panel.at[nxt], *p, 2)
-    push(panel.at[nxt, high], panel.at[nxt, high], *p, 4, beside(3))
-    push(panel.at[prev], panel.at[prev], *p, 5, partner)
-    push(panel.at[nxt], panel.at[nxt], *p, 6, partner)
-    acc[...] += product(3, core)
-    landed(panel.at[spot(3, other)], *p, 5)
-    acc[...] += product(3, other)
-    landed(panel.at[over, low], *p, 3)
-    push(panel.at[over, low], panel.at[over, low], *p, 7, partner)
-    landed(panel.at[over, high], *p, 4)
-    push(panel.at[over, high], panel.at[over, high], *p, 8, partner)
-    acc[...] += product(1, core)
-    landed(panel.at[spot(1, other)], *p, 6)
-    acc[...] += product(1, other)
-    acc[...] += product(2, core)
-    last = spot(2, other)
-    landed(panel.at[last, low], *p, 7)
-    landed(panel.at[last, high], *p, 8)
-    total = acc[...] + product(2, other)
-    for u in range(8):
-        for h in range(2):
-            part[h, u] = total[u * 128 : (u + 1) * 128, h * 128 : (h + 1) * 128].astype(BF16)
-
-    def scatter(axis, source, landing, sends, recvs, i):
-        target, device = along(axis, i)
-        push(source(target), landing.at[spots[axis]], sends, recvs, i, device)
-
-    def gathered(axis, landing, sends, recvs):
-        for i in FAR_FIRST[::-1]:
-            landed(landing.at[ring(spots[axis], 8 - i, 8)], sends, recvs, i)
+
+    def multiply(n, digits):
+        digit = lax.rem(digits, 8)
+        fetch(digit).wait()
+
+        @pl.when(n == 1)
+        def _():
+            landed(panel.at[spot(0, other)], *p, 0)
+
+        @pl.when(n == 2)
+        def _():
+            landed(panel.at[prev], *p, 1)
+            hop(3).start()
+            landed(panel.at[nxt], *p, 2)
+            hop(4).start()
+            hop(5).start()
+            hop(6).start()
+
+        @pl.when(n == 3)
+        def _():
+            landed(panel.at[spot(3, other)], *p, 5)
+
+        @pl.when(n == 4)
+        def _():
+            landed(panel.at[over, low], *p, 3)
+            hop(7).start()
+            landed(panel.at[over, high], *p, 4)
+            hop(8).start()
+
+        @pl.when(n == 5)
+        def _():
+            landed(panel.at[spot(1, other)], *p, 6)
+
+        @pl.when(n == 7)
+        def _():
+            landed(panel.at[last, low], *p, 7)
+            landed(panel.at[last, high], *p, 8)
+
+        q = place(digit)
+        acc[...] += jnp.dot(tile[q], panel[q], preferred_element_type=F32)
+        return lax.div(digits, 8)
+
+    lax.fori_loop(0, 8, multiply, table(FORWARD))
+
+    def walk(axis, source, landing, send, recv, what):
+        if what == "start":
+            def step(i):
+                target, device = along(axis, i)
+                remote(source(target), landing.at[spots[axis]], send, recv, device).start()
+
+            far_first(step)
+        else:
+            seven = landing.at[pl.ds(0, 7)]
+            whole = remote(seven, seven, send, recv, partner)
+            if what == "arrive":
+                whole.wait_recv()
+            else:
+                whole.wait_send()
 
     def u(stage, h):
         return send_u.at[stage, h], recv_u.at[stage, h]
 
     me, first, second = (y, z), ("y", "z"), ("z", "y")
-    for i in FAR_FIRST:
-        for h in range(2):
-            scatter(first[h], lambda t, h=h: part.at[h, t], got1.at[h], *u(0, h), i)
+    jobs = [
+        [(first[h], lambda t, h=h: part.at[h, t], got1.at[h]) for h in range(2)],
+        [(second[h], lambda t, h=h: sum1.at[h, t], got2.at[h]) for h in range(2)],
+        [(second[h], lambda t, h=h: mine.at[h], wide.at[h]) for h in range(2)],
+        [(first[h], lambda t, h=h: turned.at[h], users.at[h]) for h in range(2)],
+    ]
+
+    def users_step(stage, h, what):
+        walk(*jobs[stage][h], *u(stage, h), what)
+
+    for h in range(2):
+        def narrow(k, carry, h=h):
+            rows = pl.ds(pl.multiple_of(k * 128, 128), 128)
+            part[h, k] = acc[rows, h * 128 : (h + 1) * 128].astype(BF16)
+            return carry
+
+        lax.fori_loop(0, 8, narrow, 0)
+        users_step(0, h, "start")
     for h in range(2):
         got1[h, me[h]] = part[h, me[h]]
-    drain(14)
-    for h in range(2):
-        gathered(first[h], got1.at[h], *u(0, h))
+    for n in range(9):
+        hop(n).wait_send()
+    for h in range(2):
+        users_step(0, h, "arrive")
         total = got1[h, 0].astype(F32)
         for k in range(1, 8):
             total = total + got1[h, k].astype(F32)
         sum1[h] = total.reshape(8, 16, 128)
-        for i in FAR_FIRST:
-            scatter(second[h], lambda t, h=h: sum1.at[h, t], got2.at[h], *u(1, h), i)
+        users_step(1, h, "start")
         got2[h, me[1 - h]] = sum1[h, me[1 - h]]
-    drain(14)
-    for h in range(2):
-        gathered(second[h], got2.at[h], *u(1, h))
+    for h in range(2):
+        users_step(0, h, "leave")
+    for h in range(2):
+        users_step(1, h, "arrive")
         total = got2[h, 0]
         for k in range(1, 8):
             total = total + got2[h, k]
         mine[h] = total.astype(BF16)
-        for i in FAR_FIRST:
-            scatter(second[h], lambda t, h=h: mine.at[h], wide.at[h], *u(2, h), i)
+        users_step(2, h, "start")
         wide[h, me[1 - h]] = mine[h]
-    drain(14)
-
-    def up(h, d, src, dst):
-        push(src, dst, *u(3, h), d - 1, along(first[h], 1)[1])
-
-    def down(h, d, src, dst):
-        push(src, dst, *u(3, h), d + 3, along(first[h], 7)[1])
-
-    for h in range(2):
-        gathered(second[h], wide.at[h], *u(2, h))
+    for h in range(2):
+        users_step(1, h, "leave")
+
+    for h in range(2):
+        users_step(2, h, "arrive")
         turned[h] = wide[h].reshape(128, 128).astype(F32).T.astype(BF16)
-        up(h, 1, turned.at[h], users.at[h, me[h]])
-        down(h, 1, turned.at[h], users.at[h, me[h]])
+        users_step(3, h, "start")
         users[h, me[h]] = turned[h]
-    drain(4)
-    upper, lower = pl.ds(0, 64), pl.ds(64, 64)
-    for d in range(1, 4):
-        for h in range(2):
-            below = users.at[h, ring(me[h], 8 - d, 8)]
-            landed(below, *u(3, h), d - 1)
-            if d == 3:
-                below = below.at[upper]
-            up(h, d + 1, below, below)
-            above = users.at[h, ring(me[h], d, 8)]
-            landed(above, *u(3, h), d + 3)
-            if d == 3:
-                above = above.at[lower]
-            down(h, d + 1, above, above)
-    for h in range(2):
-        across = users.at[h, ring(me[h], 4, 8)]
-        landed(across.at[upper], *u(3, h), 3)
-        landed(across.at[lower], *u(3, h), 7)
-
-    def term(i, which):
+    for h in range(2):
+        users_step(2, h, "leave")
+    for h in range(2):
+        users_step(3, h, "arrive")
+
+    a, b = (send_a, recv_a), (send_b, recv_b)
+
+    def lend(i):
+        return remote(value.at[2 * i + 1], near.at[i], send_a.at[i], recv_a.at[i], partner)
+
+    moves = [
+        (pack.at[2, low], relay.at[0], beside(1)),
+        (pack.at[2, high], relay.at[1], beside(3)),
+        (pack.at[1, high], far.at[0, high], beside(1)),
+        (pack.at[3, low], far.at[1, low], beside(3)),
+        (pack.at[1, low], far.at[0, low], beside(1)),
+        (pack.at[3, high], far.at[1, high], beside(3)),
+    ]
+
+    def pass_on(n):
+        src, dst, device = moves[n]
+        return remote(src, dst, send_b.at[n], recv_b.at[n], device)
+
+    def meet(i):
+        landed(near.at[i], *a, i)
+        near[i] = value[2 * i] + near[i]
+
+    def transposed(n, digits):
+        digit = lax.rem(digits, 8)
         left = jnp.concatenate(
             [jnp.concatenate([users[h, k] for k in range(8)], axis=1) for h in range(2)], axis=0
         )
-        return jnp.dot(left, tile[spot(i, which)], preferred_element_type=F32)
-
-    a, b = (send_a, recv_a), (send_b, recv_b)
-
-    def lend(i):
-        give[i] = term(i, other)
-        push(give.at[i], near.at[i], *a, i, partner)
-
-    lend(2)
-    lend(1)
-    value = term(2, core)
-    landed(near.at[2], *a, 2)
-    pack[2] = (value + near[2]).astype(BF16)
-    push(pack.at[2, low], relay.at[0], *b, 0, beside(1))
-    push(pack.at[2, high], relay.at[1], *b, 1, beside(3))
-    lend(3)
-    value = term(1, core)
-    landed(near.at[1], *a, 1)
-    near[1] = value + near[1]
-    pack[1, HALF:] = near[1, HALF:].astype(BF16)
-    push(pack.at[1, high], far.at[0, high], *b, 2, beside(1))
-    lend(0)
-    value = term(3, core)
-    landed(near.at[3], *a, 3)
-    near[3] = value + near[3]
-    pack[3, :HALF] = near[3, :HALF].astype(BF16)
-    push(pack.at[3, low], far.at[1, low], *b, 3, beside(3))
+        value[digit] = jnp.dot(left, tile[place(digit)], preferred_element_type=F32)
+        for step, i in ((0, 2), (1, 1), (3, 3), (5, 0)):
+            @pl.when(n == step)
+            def _(i=i):
+                lend(i).start()
+
+        @pl.when(n == 2)
+        def _():
+            meet(2)
+            pack[2] = near[2].astype(BF16)
+            pass_on(0).start()
+            pass_on(1).start()
+
+        @pl.when(n == 4)
+        def _():
+            meet(1)
+            pack[1, HALF:] = near[1, HALF:].astype(BF16)
+            pass_on(2).start()
+
+        @pl.when(n == 6)
+        def _():
+            meet(3)
+            pack[3, :HALF] = near[3, :HALF].astype(BF16)
+            pass_on(3).start()
+
+        return lax.div(digits, 8)
+
+    lax.fori_loop(0, 8, transposed, table(BACKWARD))
     landed(relay.at[0], *b, 0)
     pack[1, :HALF] = (near[1, :HALF] + relay[0].astype(F32)).astype(BF16)
-    push(pack.at[1, low], far.at[0, low], *b, 4, beside(1))
+    pass_on(4).start()
     landed(relay.at[1], *b, 1)
     pack[3, HALF:] = (near[3, HALF:] + relay[1].astype(F32)).astype(BF16)
-    push(pack.at[3, high], far.at[1, high], *b, 5, beside(3))
-    value = term(0, core)
-    landed(near.at[0], *a, 0)
-    near[0] = value + near[0]
-    drain(2)
+    pass_on(5).start()
+    meet(0)
+
+    for h in range(2):
+        users_step(3, h, "leave")
+    for i in range(X):
+        lend(i).wait_send()
     landed(far.at[0, high], *b, 2)
     landed(far.at[1, low], *b, 3)
     landed(far.at[0, low], *b, 4)
@@ -353,48 +422,47 @@
     def g(n):
         return send_g.at[n], recv_g.at[n]
 
-    def move(n, axis, source, landing):
-        for i in FAR_FIRST:
-            scatter(axis, source, landing, *g(n), i)
+    spread = [
+        ("r", lambda t: cut.at[t], gram1),
+        ("y", lambda t: gsum1.at[t], gram2),
+        ("z", lambda t: gsum2, gram3),
+        ("y", lambda t: gsum3, gwide),
+        ("r", lambda t: gwide, gram_ref),
+    ]
+
+    def move(n):
+        axis, source, landing = spread[n]
+        walk(*spread[n], *g(n), "start")
         landing[spots[axis]] = source(spots[axis])[...]
-        drain(7)
-        gathered(axis, landing, *g(n))
+        if n:
+            walk(*spread[n - 1], *g(n - 1), "leave")
+        else:
+            for k in range(6):
+                pass_on(k).wait_send()
+        walk(*spread[n], *g(n), "arrive")
 
     def summed(got):
-        total = got[0]
+        total = got[0].astype(F32)
         for k in range(1, 8):
-            total = total + got[k]
+            total = total + got[k].astype(F32)
         return total
 
-    move(0, "r", lambda t: cut.at[t], gram1)
-    total = gram1[0].astype(F32)
-    for k in range(1, 8):
-        total = total + gram1[k].astype(F32)
-    gsum1[...] = total.reshape(8, 8, 128)
-    move(1, "y", lambda t: gsum1.at[t], gram2)
+    move(0)
+    gsum1[...] = summed(gram1).reshape(8, 8, 128)
+    move(1)
     gsum2[...] = summed(gram2)
-    move(2, "z", lambda t: gsum2, gram3)
+    move(2)
     gsum3[...] = summed(gram3)
-    move(3, "y", lambda t: gsum3, gwide)
-    for i in (2, 1, 3):
-        push(gwide, gram_ref.at[row], *g(4), i, beside(i))
-    push(gwide, gram_ref.at[row], *g(4), 0, partner)
-    gram_ref[row] = gwide[...]
-    drain(4)
-    for i in (3, 1, 2):
-        block = gram_ref.at[spot(4 - i, core)]
-        landed(block, *g(4), i)
-        push(block, block, *g(4), 4 + i, partner)
-    landed(gram_ref.at[spot(0, other)], *g(4), 0)
-    for i in (3, 1, 2):
-        landed(gram_ref.at[spot(4 - i, other)], *g(4), 4 + i)
-    drain()
+    move(3)
+
+    move(4)
+    walk(*spread[4], *g(4), "leave")
 
 
 def krylov(own, tile):
     cell = (8, 128)
     dma = pltpu.SemaphoreType.DMA
-    pairs = [(9,), (4, 2, 8), (X,), (6,), (5, 8)]
+    pairs = [(9,), (4, 2), (X,), (6,), (5,)]
     return pl.pallas_call(
         krylov_kernel,
         out_shape=(
@@ -415,7 +483,7 @@
             pltpu.VMEM((2, 8, 16, 128), BF16),
             pltpu.VMEM((2, 128, 128), BF16),
             pltpu.VMEM((2, 8, 128, 128), BF16),
-            pltpu.VMEM((X, 256, 256), F32),
+            pltpu.VMEM((8, 256, 256), F32),
             pltpu.VMEM((X, 256, 256), F32),
             pltpu.VMEM((X, 256, 256), BF16),
             pltpu.VMEM((2, HALF, 256), BF16),
@@ -432,7 +500,7 @@
         ]
         + [dma(shape) for shape in pairs for _ in range(2)],
         compiler_params=pltpu.CompilerParams(
-            collective_id=0, has_side_effects=True, vmem_limit_bytes=LIMIT
+            collective_id=0, has_side_effects=True, vmem_limit_bytes=ROOM
         ),
         name="krylov",
     )(own, tile)
@@ -539,7 +607,7 @@
         in_specs=[vmem(), vmem()],
         out_specs=(vmem(), vmem()),
         scratch_shapes=[pltpu.VMEM((N, N), F32), pltpu.VMEM((N, 128), F32)],
-        compiler_params=pltpu.CompilerParams(vmem_limit_bytes=LIMIT),
+        compiler_params=pltpu.CompilerParams(vmem_limit_bytes=ROOM),
         name="factor",
     )(gram, items)
 

time: 113 us -> 102 us (0.903)
  Pallas kernels: 112 us -> 100 us
    pallas_call x1, Pallas kernels: 93.3 us -> 82.7 us  [krylov(): pl.pallas_call(krylov_kernel, out_shape=(jax.ShapeDtypeStruct((256, 256),...]
where the time goes in v4:
time: 102 us; the launch traced here: 101 us
  Pallas kernels  100 us (98%)
  between operations  1.34 us (1%)
    pallas_call x1, Pallas kernels, krylov(): pl.pallas_call(krylov_kernel, out_shape=(jax.ShapeDtypeStruct((256, 256),...  82.7 us
    pallas_call x1, Pallas kernels, factor_call(): pl.pallas_call(factor_kernel, out_shape=(jax.ShapeDtypeStruct((256, 256),...  11.6 us
    pallas_call x1, Pallas kernels, dense_tile(): pl.pallas_call(dense_kernel, grid=(NB // STEP,), out_shape=jax.ShapeDtype...  5.78 us

profile of v4, /device:TPU:1, one launch (start us, length us, event | category | flops | bytes accessed | tf_op | source)
XLA Modules:
  0.0 101.4 jit_solution(6263959588417009692)
XLA Ops:
  0.6 0.0 copy-start
  1.3 5.8 %dense_tile.1.dense_ref = bf16[8,1024,256]{2,1,0:T(8,128)(2,1)} custom-call(s32[96]{0:T(128)} %bitcast.6, s32[96]{0:T(128)} %bitcast.7, s32[1]{0:T(128)} %bitcast.4.count_ref, bf16[96,128,128]{2,1,0:T(8,128)(2,1)} %bitcast.5), custom_call_target="tpu_custom_call" | custom-call | tf_op jit(solution)/shard_map/dense_tile/pallas_call | solution.py:119
  7.1 0.0 copy-done
  7.1 82.7 %krylov.1 = (f32[256,256]{1,0:T(8,128)S(1)}, f32[8,8,8,128]{3,2,1,0:T(8,128)S(1)}) custom-call(bf16[256,256]{1,0:T(8,128)(2,1)S(1)} %copy-done, bf16[8,1024,256]{2,1,0:T(8,128)(2,1)} %dense_tile.1.dense_ref), custom_call_target="tpu_custom_call" | custom-call | tf_op jit(solution)/shard_map/krylov/pallas_call | solution.py:466
  89.8 11.6 %factor.1 = (f32[256,256]{1,0:T(8,128)}, f32[256,256]{1,0:T(8,128)}) custom-call(f32[8,8,8,128]{3,2,1,0:T(8,128)S(1)} %get-tuple-element.4.gram_ref, f32[256,256]{1,0:T(8,128)S(1)} %get-tuple-element.5.items_ref), custom_call_target="tpu_custom_call" | custom-call | tf_op jit(solution)/shard_map/factor/pallas_call | solution.py:601
Async XLA Ops:
  0.6 6.5 %copy-start = (bf16[256,256]{1,0:T(8,128)(2,1)S(1)}, bf16[256,256]{1,0:T(8,128)(2,1)}, u32[]{:S(2)}) copy-start(bf16[256,256]{1,0:T(8,128)(2,1)} %own_ref.1) | copy-start | bytes 393220

commit v5 on v4

--- a/solution.py
+++ b/solution.py
@@ -63,30 +63,27 @@
     pl.semaphore_wait(barrier, total)
 
 
-def dense_kernel(rows_ref, cols_ref, count_ref, tiles_ref, out_ref, acc_ref, pack_ref, sem):
+def dense_kernel(rows_ref, cols_ref, count_ref, tiles_ref, out_ref, acc_ref, pack_ref, seen_ref, sem):
     step = pl.program_id(0)
 
     @pl.when(step == 0)
     def _():
-        acc_ref[...] = jnp.zeros_like(acc_ref)
+        def clear(k, carry):
+            seen_ref[k] = 0
+            return carry
+
+        lax.fori_loop(0, 128, clear, 0)
 
     count = count_ref[0]
 
     def group(g, carry):
-        for j in range(0, GROUP, 2):
-            spots, tiles = [], []
-            for k in range(2):
-                at = g * GROUP + j + k
-                slot = step * STEP + at
-                col = cols_ref[slot]
-                spots.append((lax.div(col, 2), lax.rem(col, 2), rows_ref[slot]))
-                tiles.append(jnp.where(slot < count, tiles_ref[at].astype(F32), 0.0))
-            same = (spots[0][0] == spots[1][0]) & (spots[0][1] == spots[1][1])
-            same = same & (spots[0][2] == spots[1][2])
-            one = acc_ref[spots[0]] + tiles[0]
-            two = jnp.where(same, one, acc_ref[spots[1]]) + tiles[1]
-            acc_ref[spots[0]] = one
-            acc_ref[spots[1]] = two
+        for j in range(GROUP):
+            at = g * GROUP + j
+            slot = step * STEP + at
+            tile = jnp.where(slot < count, tiles_ref[at].astype(F32), 0.0)
+            place = cols_ref[slot] * 8 + rows_ref[slot]
+            acc_ref[place] = jnp.where(seen_ref[place] > 0, acc_ref[place], 0.0) + tile
+            seen_ref[place] = 1
         return carry
 
     lax.fori_loop(0, STEP // GROUP, group, 0)
@@ -100,7 +97,9 @@
             def block(u, inner):
                 rows = pl.ds(pl.multiple_of(u * 128, 128), 128)
                 for e in range(2):
-                    pack_ref[q, rows, e * 128 : (e + 1) * 128] = acc_ref[q, e, u].astype(BF16)
+                    place = q * 16 + e * 8 + u
+                    total = jnp.where(seen_ref[place] > 0, acc_ref[place], 0.0)
+                    pack_ref[q, rows, e * 128 : (e + 1) * 128] = total.astype(BF16)
                 return inner
 
             lax.fori_loop(0, 8, block, 0)
@@ -123,8 +122,9 @@
         in_specs=[smem(), smem(), smem(), pl.BlockSpec((STEP, 128, 128), lambda i: (i, 0, 0))],
         out_specs=pl.BlockSpec(memory_space=pl.ANY),
         scratch_shapes=[
-            pltpu.VMEM((8, 2, 8, 128, 128), F32),
+            pltpu.VMEM((128, 128, 128), F32),
             pltpu.VMEM((8, 1024, 256), BF16),
+            pltpu.SMEM((128,), jnp.int32),
             pltpu.SemaphoreType.DMA((8,)),
         ],
         compiler_params=pltpu.CompilerParams(
@@ -517,20 +517,18 @@
                 k // 4, (k // 2 % 2) * 4 + c * 2 + k % 2
             ]
 
-    def panel(q, carry):
-        base = q * PANEL
-        rows = pl.ds(pl.multiple_of(base, PANEL), PANEL)
-        w = pltpu.roll(a_ref[rows, :], lax.rem(N - base, N), 1)
+    for base in range(0, N, PANEL):
+        w = a_ref[base : base + PANEL, :]
         d = jnp.zeros((PANEL, 128), F32)
-        for t in range(PANEL // 8):
-            low = 8 * t
+        for low in range(0, PANEL, 8):
             part = w[low:, :]
             size = PANEL - low
             lane = lax.broadcasted_iota(jnp.int32, (size, N), 1)
             sub = lax.broadcasted_iota(jnp.int32, (size, N), 0) + low
             sub1 = sub[:, :128]
+            first = base + low
             columns = [
-                jnp.broadcast_to(part[:, low + b : low + b + 1], (size, 128)) for b in range(8)
+                jnp.broadcast_to(part[:, first + b : first + b + 1], (size, 128)) for b in range(8)
             ]
             d_part = d[low:, :]
             for a in range(0, 8, 2):
@@ -548,12 +546,12 @@
                     next_top = columns[b][a + 1 : a + 2, :] - ratio * top
                     columns[b] = columns[b] - m1 * top - m2 * next_top
                 lane1 = lane[:1]
-                line1 = jnp.where(lane1 == r, 1.0, part[a : a + 1, :])
+                line1 = jnp.where(lane1 == base + r, 1.0, part[a : a + 1, :])
                 ratio2 = jnp.concatenate([ratio, ratio], axis=1)
-                line2 = jnp.where(lane1 == r, 0.0, part[a + 1 : a + 2, :]) - ratio2 * line1
-                line1 = jnp.where(lane1 == r + 1, 0.0, line1)
-                line2 = jnp.where(lane1 == r + 1, 1.0, line2)
-                gone = ((lane == r) & (sub > r)) | ((lane == r + 1) & (sub > r + 1))
+                line2 = jnp.where(lane1 == base + r, 0.0, part[a + 1 : a + 2, :]) - ratio2 * line1
+                line1 = jnp.where(lane1 == base + r + 1, 0.0, line1)
+                line2 = jnp.where(lane1 == base + r + 1, 1.0, line2)
+                gone = ((lane == base + r) & (sub > r)) | ((lane == base + r + 1) & (sub > r + 1))
                 part = (
                     jnp.where(gone, 0.0, part)
                     - jnp.concatenate([m1, m1], axis=1) * line1
@@ -563,26 +561,23 @@
                 d_part = jnp.where(sub1 == r + 1, p22 - ratio * p12, d_part)
             w = part if low == 0 else jnp.concatenate([w[:low], part], axis=0)
             d = d_part if low == 0 else jnp.concatenate([d[:low], d_part], axis=0)
-        d_ref[rows, :] = d
+        a_ref[base : base + PANEL, :] = w
+        d_ref[base : base + PANEL, :] = d
+        after = base + PANEL
+        if after == N:
+            break
         lane = lax.broadcasted_iota(jnp.int32, (PANEL, N), 1)
-        sub = lax.broadcasted_iota(jnp.int32, (PANEL, N), 0)
-        d2 = jnp.concatenate([d, d], axis=1)
-        ahead = (lane >= PANEL) & (lane < N - base)
-        scaled = jnp.where(ahead, w / d2, 0.0)
-        right = jnp.where((lane < PANEL) & (lane >= sub), jnp.where(lane == sub, 1.0, 0.0), w)
-        a_ref[rows, :] = pltpu.roll(w, base, 1)
-        scaled = pltpu.roll(scaled, base, 1)
-        right = pltpu.roll(right, base, 1)
-        update = lax.dot_general(
-            scaled, right, (((0,), (0,)), ((), ())), precision=HIGH, preferred_element_type=F32
-        )
-        full_lane = lax.broadcasted_iota(jnp.int32, (N, N), 1)
-        full_sub = lax.broadcasted_iota(jnp.int32, (N, N), 0)
-        done = (full_sub >= base + PANEL) & (full_lane >= base) & (full_lane < base + PANEL)
-        a_ref[...] = jnp.where(done, 0.0, a_ref[...]) - update
-        return carry
-
-    lax.fori_loop(0, N // PANEL, panel, 0)
+        sub = lax.broadcasted_iota(jnp.int32, (PANEL, N), 0) + base
+        scaled = jnp.where(lane >= after, w / jnp.concatenate([d, d], axis=1), 0.0).T
+        inside = (lane < after) & (lane >= sub)
+        right = jnp.where(inside, jnp.where(lane == sub, 1.0, 0.0), w)
+        for top, bottom in ((after, after + PANEL), (after + PANEL, N)):
+            if top < bottom:
+                lane = lax.broadcasted_iota(jnp.int32, (bottom - top, N), 1)
+                kept = jnp.where((lane >= base) & (lane < after), 0.0, a_ref[top:bottom, :])
+                a_ref[top:bottom, :] = kept - jnp.dot(
+                    scaled[top:bottom], right, precision=HIGH, preferred_element_type=F32
+                )
 
     lane = lax.broadcasted_iota(jnp.int32, (N, N), 1)
     sub = lax.broadcasted_iota(jnp.int32, (N, N), 0)

time: 102 us -> 99.3 us (0.974)
  Pallas kernels: 100 us -> 97.8 us
    pallas_call x1, Pallas kernels: 11.6 us -> 8.6 us  [factor_call(): pl.pallas_call(factor_kernel, out_shape=(jax.ShapeDtypeStruct((256, 256),...]
where the time goes in v5:
time: 99.3 us; the launch traced here: 99.1 us
  Pallas kernels  97.8 us (98%)
  between operations  1.34 us (1%)
    pallas_call x1, Pallas kernels, krylov(): pl.pallas_call(krylov_kernel, out_shape=(jax.ShapeDtypeStruct((256, 256),...  82.8 us
    pallas_call x1, Pallas kernels, factor_call(): pl.pallas_call(factor_kernel, out_shape=(jax.ShapeDtypeStruct((256, 256),...  8.6 us
    pallas_call x1, Pallas kernels, dense_tile(): pl.pallas_call(dense_kernel, grid=(NB // STEP,), out_shape=jax.ShapeDtype...  6.42 us

profile of v5, /device:TPU:1, one launch (start us, length us, event | category | flops | bytes accessed | tf_op | source)
XLA Modules:
  0.0 99.1 jit_solution(15376995028015127434)
XLA Ops:
  0.6 0.0 copy-start
  1.3 6.4 %dense_tile.1.dense_ref = bf16[8,1024,256]{2,1,0:T(8,128)(2,1)} custom-call(s32[96]{0:T(128)} %bitcast.6, s32[96]{0:T(128)} %bitcast.7, s32[1]{0:T(128)} %bitcast.4.count_ref, bf16[96,128,128]{2,1,0:T(8,128)(2,1)} %bitcast.5), custom_call_target="tpu_custom_call" | custom-call | tf_op jit(solution)/shard_map/dense_tile/pallas_call | solution.py:118
  7.7 0.0 copy-done
  7.8 82.8 %krylov.1 = (f32[256,256]{1,0:T(8,128)S(1)}, f32[8,8,8,128]{3,2,1,0:T(8,128)S(1)}) custom-call(bf16[256,256]{1,0:T(8,128)(2,1)S(1)} %copy-done, bf16[8,1024,256]{2,1,0:T(8,128)(2,1)} %dense_tile.1.dense_ref), custom_call_target="tpu_custom_call" | custom-call | tf_op jit(solution)/shard_map/krylov/pallas_call | solution.py:466
  90.6 8.6 %factor.1 = (f32[256,256]{1,0:T(8,128)}, f32[256,256]{1,0:T(8,128)}) custom-call(f32[8,8,8,128]{3,2,1,0:T(8,128)S(1)} %get-tuple-element.4.gram_ref, f32[256,256]{1,0:T(8,128)S(1)} %get-tuple-element.5.items_ref), custom_call_target="tpu_custom_call" | custom-call | tf_op jit(solution)/shard_map/factor/pallas_call | solution.py:596
Async XLA Ops:
  0.6 7.1 %copy-start = (bf16[256,256]{1,0:T(8,128)(2,1)S(1)}, bf16[256,256]{1,0:T(8,128)(2,1)}, u32[]{:S(2)}) copy-start(bf16[256,256]{1,0:T(8,128)(2,1)} %own_ref.1) | copy-start | bytes 393220

commit v6 on v5

--- a/solution.py
+++ b/solution.py
@@ -63,16 +63,12 @@
     pl.semaphore_wait(barrier, total)
 
 
-def dense_kernel(rows_ref, cols_ref, count_ref, tiles_ref, out_ref, acc_ref, pack_ref, seen_ref, sem):
+def dense_kernel(rows_ref, cols_ref, count_ref, tiles_ref, out_ref, acc_ref, pack_ref, sem):
     step = pl.program_id(0)
 
     @pl.when(step == 0)
     def _():
-        def clear(k, carry):
-            seen_ref[k] = 0
-            return carry
-
-        lax.fori_loop(0, 128, clear, 0)
+        acc_ref[...] = jnp.zeros_like(acc_ref)
 
     count = count_ref[0]
 
@@ -81,9 +77,8 @@
             at = g * GROUP + j
             slot = step * STEP + at
             tile = jnp.where(slot < count, tiles_ref[at].astype(F32), 0.0)
-            place = cols_ref[slot] * 8 + rows_ref[slot]
-            acc_ref[place] = jnp.where(seen_ref[place] > 0, acc_ref[place], 0.0) + tile
-            seen_ref[place] = 1
+            col = cols_ref[slot]
+            acc_ref[lax.div(col, 2), lax.rem(col, 2), rows_ref[slot]] += tile
         return carry
 
     lax.fori_loop(0, STEP // GROUP, group, 0)
@@ -97,9 +92,7 @@
             def block(u, inner):
                 rows = pl.ds(pl.multiple_of(u * 128, 128), 128)
                 for e in range(2):
-                    place = q * 16 + e * 8 + u
-                    total = jnp.where(seen_ref[place] > 0, acc_ref[place], 0.0)
-                    pack_ref[q, rows, e * 128 : (e + 1) * 128] = total.astype(BF16)
+                    pack_ref[q, rows, e * 128 : (e + 1) * 128] = acc_ref[q, e, u].astype(BF16)
                 return inner
 
             lax.fori_loop(0, 8, block, 0)
@@ -122,9 +115,8 @@
         in_specs=[smem(), smem(), smem(), pl.BlockSpec((STEP, 128, 128), lambda i: (i, 0, 0))],
         out_specs=pl.BlockSpec(memory_space=pl.ANY),
         scratch_shapes=[
-            pltpu.VMEM((128, 128, 128), F32),
+            pltpu.VMEM((8, 2, 8, 128, 128), F32),
             pltpu.VMEM((8, 1024, 256), BF16),
-            pltpu.SMEM((128,), jnp.int32),
             pltpu.SemaphoreType.DMA((8,)),
         ],
         compiler_params=pltpu.CompilerParams(
@@ -145,7 +137,7 @@
 
 def krylov_kernel(
     own_ref, dense_ref, items_ref, gram_ref,
-    tile, panel, acc, part, got1, sum1, got2, mine, wide, turned, users,
+    tile, panel, turned, acc, part, got1, sum1, got2, mine, wide, whole, users,
     value, near, pack, relay, far, cut, gram1, gsum1, gram2, gsum2, gram3, gsum3, gwide,
     load, send_p, recv_p, send_u, recv_u, send_a, recv_a, send_b, recv_b, send_g, recv_g,
 ):
@@ -181,9 +173,8 @@
         fetch(lax.rem(digits, 8)).start()
         return lax.div(digits, 8)
 
-    mine_copy = pltpu.make_async_copy(own_ref, panel.at[row], load.at[8])
-    mine_copy.start()
     lax.fori_loop(0, 8, fetch_next, table(FORWARD))
+    turned[...] = own_ref[...].astype(F32).T.astype(BF16)
 
     greet([(8, lambda i, axis=axis: along(axis, i)[1]) for axis in "ryz"])
 
@@ -201,9 +192,9 @@
     last = spot(2, other)
     p = (send_p, recv_p)
     hops = [
-        (own_ref, panel.at[row], partner),
-        (own_ref, panel.at[row], beside(1)),
-        (own_ref, panel.at[row], beside(3)),
+        (turned, panel.at[row], partner),
+        (turned, panel.at[row], beside(1)),
+        (turned, panel.at[row], beside(3)),
         (panel.at[prev, low], panel.at[prev, low], beside(1)),
         (panel.at[nxt, high], panel.at[nxt, high], beside(3)),
         (panel.at[prev], panel.at[prev], partner),
@@ -218,8 +209,8 @@
 
     for n in (1, 2, 0):
         hop(n).start()
+    panel[row] = turned[...]
     acc[...] = jnp.zeros_like(acc)
-    mine_copy.wait()
 
     def multiply(n, digits):
         digit = lax.rem(digits, 8)
@@ -259,7 +250,9 @@
             landed(panel.at[last, high], *p, 8)
 
         q = place(digit)
-        acc[...] += jnp.dot(tile[q], panel[q], preferred_element_type=F32)
+        acc[...] += lax.dot_general(
+            panel[q], tile[q], (((1,), (1,)), ((), ())), preferred_element_type=F32
+        )
         return lax.div(digits, 8)
 
     lax.fori_loop(0, 8, multiply, table(FORWARD))
@@ -279,61 +272,54 @@
             else:
                 whole.wait_send()
 
-    def u(stage, h):
-        return send_u.at[stage, h], recv_u.at[stage, h]
-
-    me, first, second = (y, z), ("y", "z"), ("z", "y")
+    me, first, second = (y, z, y, z), ("y", "z", "y", "z"), ("z", "y", "z", "y")
+    them = (z, y, z, y)
     jobs = [
-        [(first[h], lambda t, h=h: part.at[h, t], got1.at[h]) for h in range(2)],
-        [(second[h], lambda t, h=h: sum1.at[h, t], got2.at[h]) for h in range(2)],
-        [(second[h], lambda t, h=h: mine.at[h], wide.at[h]) for h in range(2)],
-        [(first[h], lambda t, h=h: turned.at[h], users.at[h]) for h in range(2)],
+        [(first[h], lambda t, h=h: part.at[h, t], got1.at[h]) for h in range(4)],
+        [(second[h], lambda t, h=h: sum1.at[h, t], got2.at[h]) for h in range(4)],
+        [(second[h], lambda t, h=h: mine.at[h], wide.at[h]) for h in range(4)],
+        [(first[h], lambda t, h=h: whole.at[h], users.at[h]) for h in range(4)],
     ]
 
     def users_step(stage, h, what):
-        walk(*jobs[stage][h], *u(stage, h), what)
-
-    for h in range(2):
-        def narrow(k, carry, h=h):
-            rows = pl.ds(pl.multiple_of(k * 128, 128), 128)
-            part[h, k] = acc[rows, h * 128 : (h + 1) * 128].astype(BF16)
-            return carry
-
-        lax.fori_loop(0, 8, narrow, 0)
+        walk(*jobs[stage][h], send_u.at[stage, h], recv_u.at[stage, h], what)
+
+    def summed(got):
+        total = got[0].astype(F32)
+        for k in range(1, 8):
+            total = total + got[k].astype(F32)
+        return total
+
+    for h in range(4):
+        for k in range(8):
+            part[h, k] = acc[h * 64 : (h + 1) * 64, k * 128 : (k + 1) * 128].astype(BF16)
         users_step(0, h, "start")
-    for h in range(2):
+    for h in range(4):
         got1[h, me[h]] = part[h, me[h]]
     for n in range(9):
         hop(n).wait_send()
-    for h in range(2):
+    for h in range(4):
         users_step(0, h, "arrive")
-        total = got1[h, 0].astype(F32)
-        for k in range(1, 8):
-            total = total + got1[h, k].astype(F32)
-        sum1[h] = total.reshape(8, 16, 128)
+        sum1[h] = summed(got1.at[h]).reshape(8, 8, 128)
         users_step(1, h, "start")
-        got2[h, me[1 - h]] = sum1[h, me[1 - h]]
-    for h in range(2):
+        got2[h, them[h]] = sum1[h, them[h]]
+    for h in range(4):
         users_step(0, h, "leave")
-    for h in range(2):
+    for h in range(4):
         users_step(1, h, "arrive")
-        total = got2[h, 0]
-        for k in range(1, 8):
-            total = total + got2[h, k]
-        mine[h] = total.astype(BF16)
+        mine[h] = summed(got2.at[h])
         users_step(2, h, "start")
-        wide[h, me[1 - h]] = mine[h]
-    for h in range(2):
+        wide[h, them[h]] = mine[h]
+    for h in range(4):
         users_step(1, h, "leave")
-
-    for h in range(2):
+    for h in range(4):
         users_step(2, h, "arrive")
-        turned[h] = wide[h].reshape(128, 128).astype(F32).T.astype(BF16)
+        whole[h] = wide[h].reshape(64, 128).astype(BF16)
         users_step(3, h, "start")
-        users[h, me[h]] = turned[h]
-    for h in range(2):
+        users[h, me[h]] = whole[h]
+    for h in range(4):
         users_step(2, h, "leave")
-    for h in range(2):
+    for h in range(4):
         users_step(3, h, "arrive")
 
     a, b = (send_a, recv_a), (send_b, recv_b)
@@ -361,7 +347,7 @@
     def transposed(n, digits):
         digit = lax.rem(digits, 8)
         left = jnp.concatenate(
-            [jnp.concatenate([users[h, k] for k in range(8)], axis=1) for h in range(2)], axis=0
+            [jnp.concatenate([users[h, k] for k in range(8)], axis=1) for h in range(4)], axis=0
         )
         value[digit] = jnp.dot(left, tile[place(digit)], preferred_element_type=F32)
         for step, i in ((0, 2), (1, 1), (3, 3), (5, 0)):
@@ -399,7 +385,7 @@
     pass_on(5).start()
     meet(0)
 
-    for h in range(2):
+    for h in range(4):
         users_step(3, h, "leave")
     for i in range(X):
         lend(i).wait_send()
@@ -441,12 +427,6 @@
                 pass_on(k).wait_send()
         walk(*spread[n], *g(n), "arrive")
 
-    def summed(got):
-        total = got[0].astype(F32)
-        for k in range(1, 8):
-            total = total + got[k].astype(F32)
-        return total
-
     move(0)
     gsum1[...] = summed(gram1).reshape(8, 8, 128)
     move(1)
@@ -462,27 +442,28 @@
 def krylov(own, tile):
     cell = (8, 128)
     dma = pltpu.SemaphoreType.DMA
-    pairs = [(9,), (4, 2), (X,), (6,), (5,)]
+    pairs = [(9,), (4, 4), (X,), (6,), (5,)]
     return pl.pallas_call(
         krylov_kernel,
         out_shape=(
             jax.ShapeDtypeStruct((256, 256), F32),
             jax.ShapeDtypeStruct((8, 8) + cell, F32),
         ),
-        in_specs=[pl.BlockSpec(memory_space=pl.ANY), pl.BlockSpec(memory_space=pl.ANY)],
+        in_specs=[vmem(), pl.BlockSpec(memory_space=pl.ANY)],
         out_specs=(vmem(), vmem()),
         scratch_shapes=[
             pltpu.VMEM((8, 1024, 256), BF16),
             pltpu.VMEM((8, 256, 256), BF16),
-            pltpu.VMEM((1024, 256), F32),
-            pltpu.VMEM((2, 8, 128, 128), BF16),
-            pltpu.VMEM((2, 8, 128, 128), BF16),
-            pltpu.VMEM((2, 8, 16, 128), F32),
-            pltpu.VMEM((2, 8, 16, 128), F32),
-            pltpu.VMEM((2, 16, 128), BF16),
-            pltpu.VMEM((2, 8, 16, 128), BF16),
-            pltpu.VMEM((2, 128, 128), BF16),
-            pltpu.VMEM((2, 8, 128, 128), BF16),
+            pltpu.VMEM((256, 256), BF16),
+            pltpu.VMEM((256, 1024), F32),
+            pltpu.VMEM((4, 8, 64, 128), BF16),
+            pltpu.VMEM((4, 8, 64, 128), BF16),
+            pltpu.VMEM((4, 8) + cell, F32),
+            pltpu.VMEM((4, 8) + cell, F32),
+            pltpu.VMEM((4,) + cell, F32),
+            pltpu.VMEM((4, 8) + cell, F32),
+            pltpu.VMEM((4, 64, 128), BF16),
+            pltpu.VMEM((4, 8, 64, 128), BF16),
             pltpu.VMEM((8, 256, 256), F32),
             pltpu.VMEM((X, 256, 256), F32),
             pltpu.VMEM((X, 256, 256), BF16),
@@ -496,7 +477,7 @@
             pltpu.VMEM((8,) + cell, F32),
             pltpu.VMEM(cell, F32),
             pltpu.VMEM((8,) + cell, F32),
-            dma((9,)),
+            dma((8,)),
         ]
         + [dma(shape) for shape in pairs for _ in range(2)],
         compiler_params=pltpu.CompilerParams(

time: 99.3 us -> 98.2 us (0.989)
  Pallas kernels: 97.8 us -> 96.7 us
where the time goes in v6:
time: 98.2 us; the launch traced here: 98 us
  Pallas kernels  96.7 us (98%)
  between operations  1.34 us (1%)
    pallas_call x1, Pallas kernels, krylov(): pl.pallas_call(krylov_kernel, out_shape=(jax.ShapeDtypeStruct((256, 256),...  82.3 us
    pallas_call x1, Pallas kernels, factor_call(): pl.pallas_call(factor_kernel, out_shape=(jax.ShapeDtypeStruct((256, 256),...  8.59 us
    pallas_call x1, Pallas kernels, dense_tile(): pl.pallas_call(dense_kernel, grid=(NB // STEP,), out_shape=jax.ShapeDtype...  5.76 us

profile of v6, /device:TPU:1, one launch (start us, length us, event | category | flops | bytes accessed | tf_op | source)
XLA Modules:
  0.0 98.0 jit_solution(1158797756333127568)
XLA Ops:
  0.6 0.0 copy-start
  1.3 5.8 %dense_tile.1.dense_ref = bf16[8,1024,256]{2,1,0:T(8,128)(2,1)} custom-call(s32[96]{0:T(128)} %bitcast.6, s32[96]{0:T(128)} %bitcast.7, s32[1]{0:T(128)} %bitcast.4.count_ref, bf16[96,128,128]{2,1,0:T(8,128)(2,1)} %bitcast.5), custom_call_target="tpu_custom_call" | custom-call | tf_op jit(solution)/shard_map/dense_tile/pallas_call | solution.py:111
  7.1 0.0 copy-done
  7.1 82.3 %krylov.1 = (f32[256,256]{1,0:T(8,128)S(1)}, f32[8,8,8,128]{3,2,1,0:T(8,128)S(1)}) custom-call(bf16[256,256]{1,0:T(8,128)(2,1)S(1)} %copy-done, bf16[8,1024,256]{2,1,0:T(8,128)(2,1)} %dense_tile.1.dense_ref), custom_call_target="tpu_custom_call" | custom-call | tf_op jit(solution)/shard_map/krylov/pallas_call | solution.py:446
  89.4 8.6 %factor.1 = (f32[256,256]{1,0:T(8,128)}, f32[256,256]{1,0:T(8,128)}) custom-call(f32[8,8,8,128]{3,2,1,0:T(8,128)S(1)} %get-tuple-element.4.gram_ref, f32[256,256]{1,0:T(8,128)S(1)} %get-tuple-element.5.items_ref), custom_call_target="tpu_custom_call" | custom-call | tf_op jit(solution)/shard_map/factor/pallas_call | solution.py:577
Async XLA Ops:
  0.6 6.5 %copy-start = (bf16[256,256]{1,0:T(8,128)(2,1)S(1)}, bf16[256,256]{1,0:T(8,128)(2,1)}, u32[]{:S(2)}) copy-start(bf16[256,256]{1,0:T(8,128)(2,1)} %own_ref.1) | copy-start | bytes 393220

commit v7 on v6

--- a/solution.py
+++ b/solution.py
@@ -51,7 +51,6 @@
 
 def greet(makers):
     barrier = pltpu.get_barrier_semaphore()
-    total = 0
     for count, device in makers:
         each(
             count,
@@ -59,8 +58,6 @@
                 barrier, inc=1, device_id=device(i), device_id_type=MESH
             ),
         )
-        total += count - 1
-    pl.semaphore_wait(barrier, total)
 
 
 def dense_kernel(rows_ref, cols_ref, count_ref, tiles_ref, out_ref, acc_ref, pack_ref, sem):
@@ -138,7 +135,7 @@
 def krylov_kernel(
     own_ref, dense_ref, items_ref, gram_ref,
     tile, panel, turned, acc, part, got1, sum1, got2, mine, wide, whole, users,
-    value, near, pack, relay, far, cut, gram1, gsum1, gram2, gsum2, gram3, gsum3, gwide,
+    value, near, pack, far, cut, gram1, gsum1, gram2, gsum2, gram3, gsum3, gwide,
     load, send_p, recv_p, send_u, recv_u, send_a, recv_a, send_b, recv_b, send_g, recv_g,
 ):
     row, col, y, z = places()
@@ -146,7 +143,6 @@
     other = 1 - core
     partner = (chip * 2 + other, col)
     spots = {"r": row, "y": y, "z": z}
-    low, high = pl.ds(0, HALF), pl.ds(HALF, HALF)
 
     def spot(i, which):
         return ring(chip, i, X) * 2 + which
@@ -174,9 +170,9 @@
         return lax.div(digits, 8)
 
     lax.fori_loop(0, 8, fetch_next, table(FORWARD))
+    greet([(8, lambda i, axis=axis: along(axis, i)[1]) for axis in "ryz"])
     turned[...] = own_ref[...].astype(F32).T.astype(BF16)
-
-    greet([(8, lambda i, axis=axis: along(axis, i)[1]) for axis in "ryz"])
+    pl.semaphore_wait(pltpu.get_barrier_semaphore(), 21)
 
     def landed(dst, sends, recvs, n):
         remote(dst, dst, sends.at[n], recvs.at[n], partner).wait_recv()
@@ -188,26 +184,20 @@
 
         lax.fori_loop(0, 7, step, 0)
 
-    prev, nxt, over = spot(3, core), spot(1, core), spot(2, core)
-    last = spot(2, other)
     p = (send_p, recv_p)
-    hops = [
-        (turned, panel.at[row], partner),
-        (turned, panel.at[row], beside(1)),
-        (turned, panel.at[row], beside(3)),
-        (panel.at[prev, low], panel.at[prev, low], beside(1)),
-        (panel.at[nxt, high], panel.at[nxt, high], beside(3)),
-        (panel.at[prev], panel.at[prev], partner),
-        (panel.at[nxt], panel.at[nxt], partner),
-        (panel.at[over, low], panel.at[over, low], partner),
-        (panel.at[over, high], panel.at[over, high], partner),
-    ]
+    hops = [(turned, panel.at[row], partner)]
+    hops += [(turned, panel.at[row], beside(i)) for i in (1, 2, 3)]
+    hops += [(panel.at[spot(X - i, core)], panel.at[spot(X - i, core)], partner) for i in (1, 2, 3)]
+
+    def came(n):
+        chips, which = (0, other) if n == 0 else (X - n, core) if n < X else (2 * X - 1 - n, other)
+        landed(panel.at[spot(chips, which)], *p, n)
 
     def hop(n):
         src, dst, device = hops[n]
         return remote(src, dst, send_p.at[n], recv_p.at[n], device)
 
-    for n in (1, 2, 0):
+    for n in (2, 1, 3, 0):
         hop(n).start()
     panel[row] = turned[...]
     acc[...] = jnp.zeros_like(acc)
@@ -218,36 +208,31 @@
 
         @pl.when(n == 1)
         def _():
-            landed(panel.at[spot(0, other)], *p, 0)
+            came(0)
 
         @pl.when(n == 2)
         def _():
-            landed(panel.at[prev], *p, 1)
-            hop(3).start()
-            landed(panel.at[nxt], *p, 2)
+            came(1)
             hop(4).start()
-            hop(5).start()
+            came(3)
             hop(6).start()
 
         @pl.when(n == 3)
         def _():
-            landed(panel.at[spot(3, other)], *p, 5)
+            came(4)
 
         @pl.when(n == 4)
         def _():
-            landed(panel.at[over, low], *p, 3)
-            hop(7).start()
-            landed(panel.at[over, high], *p, 4)
-            hop(8).start()
+            came(2)
+            hop(5).start()
 
         @pl.when(n == 5)
         def _():
-            landed(panel.at[spot(1, other)], *p, 6)
+            came(6)
 
         @pl.when(n == 7)
         def _():
-            landed(panel.at[last, low], *p, 7)
-            landed(panel.at[last, high], *p, 8)
+            came(5)
 
         q = place(digit)
         acc[...] += lax.dot_general(
@@ -257,20 +242,17 @@
 
     lax.fori_loop(0, 8, multiply, table(FORWARD))
 
-    def walk(axis, source, landing, send, recv, what):
-        if what == "start":
-            def step(i):
+    def launch(copies):
+        def step(i):
+            for axis, source, landing, send, recv in copies:
                 target, device = along(axis, i)
                 remote(source(target), landing.at[spots[axis]], send, recv, device).start()
 
-            far_first(step)
-        else:
-            seven = landing.at[pl.ds(0, 7)]
-            whole = remote(seven, seven, send, recv, partner)
-            if what == "arrive":
-                whole.wait_recv()
-            else:
-                whole.wait_send()
+        far_first(step)
+
+    def seven(landing, send, recv):
+        part_of = landing.at[pl.ds(0, 7)]
+        return remote(part_of, part_of, send, recv, partner)
 
     me, first, second = (y, z, y, z), ("y", "z", "y", "z"), ("z", "y", "z", "y")
     them = (z, y, z, y)
@@ -281,8 +263,15 @@
         [(first[h], lambda t, h=h: whole.at[h], users.at[h]) for h in range(4)],
     ]
 
-    def users_step(stage, h, what):
-        walk(*jobs[stage][h], send_u.at[stage, h], recv_u.at[stage, h], what)
+    def users_start(stage, quarters):
+        launch([jobs[stage][h] + (send_u.at[stage, h], recv_u.at[stage, h]) for h in quarters])
+
+    def users_all(stage, h):
+        return seven(jobs[stage][h][2], send_u.at[stage, h], recv_u.at[stage, h])
+
+    def users_left(stage):
+        for h in range(4):
+            users_all(stage, h).wait_send()
 
     def summed(got):
         total = got[0].astype(F32)
@@ -290,58 +279,51 @@
             total = total + got[k].astype(F32)
         return total
 
-    for h in range(4):
-        for k in range(8):
-            part[h, k] = acc[h * 64 : (h + 1) * 64, k * 128 : (k + 1) * 128].astype(BF16)
-        users_step(0, h, "start")
+    pairs = ((0, 1), (2, 3))
+    for pair in pairs:
+        for h in pair:
+            for k in range(8):
+                part[h, k] = acc[h * 64 : (h + 1) * 64, k * 128 : (k + 1) * 128].astype(BF16)
+        users_start(0, pair)
     for h in range(4):
         got1[h, me[h]] = part[h, me[h]]
-    for n in range(9):
+    for n in range(7):
         hop(n).wait_send()
+    for pair in pairs:
+        for h in pair:
+            users_all(0, h).wait_recv()
+            sum1[h] = summed(got1.at[h]).reshape(8, 8, 128)
+        users_start(1, pair)
+        for h in pair:
+            got2[h, them[h]] = sum1[h, them[h]]
+    users_left(0)
+    for pair in pairs:
+        for h in pair:
+            users_all(1, h).wait_recv()
+            mine[h] = summed(got2.at[h])
+        users_start(2, pair)
+        for h in pair:
+            wide[h, them[h]] = mine[h]
+    users_left(1)
+    for pair in pairs:
+        for h in pair:
+            users_all(2, h).wait_recv()
+            whole[h] = wide[h].reshape(64, 128).astype(BF16)
+        users_start(3, pair)
+        for h in pair:
+            users[h, me[h]] = whole[h]
+    users_left(2)
     for h in range(4):
-        users_step(0, h, "arrive")
-        sum1[h] = summed(got1.at[h]).reshape(8, 8, 128)
-        users_step(1, h, "start")
-        got2[h, them[h]] = sum1[h, them[h]]
-    for h in range(4):
-        users_step(0, h, "leave")
-    for h in range(4):
-        users_step(1, h, "arrive")
-        mine[h] = summed(got2.at[h])
-        users_step(2, h, "start")
-        wide[h, them[h]] = mine[h]
-    for h in range(4):
-        users_step(1, h, "leave")
-    for h in range(4):
-        users_step(2, h, "arrive")
-        whole[h] = wide[h].reshape(64, 128).astype(BF16)
-        users_step(3, h, "start")
-        users[h, me[h]] = whole[h]
-    for h in range(4):
-        users_step(2, h, "leave")
-    for h in range(4):
-        users_step(3, h, "arrive")
-
-    a, b = (send_a, recv_a), (send_b, recv_b)
+        users_all(3, h).wait_recv()
 
     def lend(i):
         return remote(value.at[2 * i + 1], near.at[i], send_a.at[i], recv_a.at[i], partner)
 
-    moves = [
-        (pack.at[2, low], relay.at[0], beside(1)),
-        (pack.at[2, high], relay.at[1], beside(3)),
-        (pack.at[1, high], far.at[0, high], beside(1)),
-        (pack.at[3, low], far.at[1, low], beside(3)),
-        (pack.at[1, low], far.at[0, low], beside(1)),
-        (pack.at[3, high], far.at[1, high], beside(3)),
-    ]
-
-    def pass_on(n):
-        src, dst, device = moves[n]
-        return remote(src, dst, send_b.at[n], recv_b.at[n], device)
+    def pass_on(i):
+        return remote(pack.at[i], far.at[i], send_b.at[i], recv_b.at[i], beside(i))
 
     def meet(i):
-        landed(near.at[i], *a, i)
+        landed(near.at[i], send_a, recv_a, i)
         near[i] = value[2 * i] + near[i]
 
     def transposed(n, digits):
@@ -355,45 +337,24 @@
             def _(i=i):
                 lend(i).start()
 
-        @pl.when(n == 2)
-        def _():
-            meet(2)
-            pack[2] = near[2].astype(BF16)
-            pass_on(0).start()
-            pass_on(1).start()
-
-        @pl.when(n == 4)
-        def _():
-            meet(1)
-            pack[1, HALF:] = near[1, HALF:].astype(BF16)
-            pass_on(2).start()
-
-        @pl.when(n == 6)
-        def _():
-            meet(3)
-            pack[3, :HALF] = near[3, :HALF].astype(BF16)
-            pass_on(3).start()
+        for step, i in ((3, 2), (5, 1), (6, 3)):
+            @pl.when(n == step)
+            def _(i=i):
+                meet(i)
+                pack[i] = near[i].astype(BF16)
+                pass_on(i).start()
 
         return lax.div(digits, 8)
 
     lax.fori_loop(0, 8, transposed, table(BACKWARD))
-    landed(relay.at[0], *b, 0)
-    pack[1, :HALF] = (near[1, :HALF] + relay[0].astype(F32)).astype(BF16)
-    pass_on(4).start()
-    landed(relay.at[1], *b, 1)
-    pack[3, HALF:] = (near[3, HALF:] + relay[1].astype(F32)).astype(BF16)
-    pass_on(5).start()
     meet(0)
-
-    for h in range(4):
-        users_step(3, h, "leave")
+    users_left(3)
     for i in range(X):
         lend(i).wait_send()
-    landed(far.at[0, high], *b, 2)
-    landed(far.at[1, low], *b, 3)
-    landed(far.at[0, low], *b, 4)
-    landed(far.at[1, high], *b, 5)
-    items = near[0] + far[0].astype(F32) + far[1].astype(F32)
+    items = near[0]
+    for i in (1, 3, 2):
+        landed(far.at[i], send_b, recv_b, i)
+        items = items + far[i].astype(F32)
     items_ref[...] = items
 
     gram = lax.dot_general(
@@ -405,9 +366,6 @@
                 16 * k : 16 * k + 16, 128 * c : 128 * c + 128
             ].astype(BF16)
 
-    def g(n):
-        return send_g.at[n], recv_g.at[n]
-
     spread = [
         ("r", lambda t: cut.at[t], gram1),
         ("y", lambda t: gsum1.at[t], gram2),
@@ -416,16 +374,19 @@
         ("r", lambda t: gwide, gram_ref),
     ]
 
+    def spread_all(n):
+        return seven(spread[n][2], send_g.at[n], recv_g.at[n])
+
     def move(n):
         axis, source, landing = spread[n]
-        walk(*spread[n], *g(n), "start")
+        launch([spread[n] + (send_g.at[n], recv_g.at[n])])
         landing[spots[axis]] = source(spots[axis])[...]
         if n:
-            walk(*spread[n - 1], *g(n - 1), "leave")
+            spread_all(n - 1).wait_send()
         else:
-            for k in range(6):
-                pass_on(k).wait_send()
-        walk(*spread[n], *g(n), "arrive")
+            for i in (1, 2, 3):
+                pass_on(i).wait_send()
+        spread_all(n).wait_recv()
 
     move(0)
     gsum1[...] = summed(gram1).reshape(8, 8, 128)
@@ -436,13 +397,13 @@
     move(3)
 
     move(4)
-    walk(*spread[4], *g(4), "leave")
+    spread_all(4).wait_send()
 
 
 def krylov(own, tile):
     cell = (8, 128)
     dma = pltpu.SemaphoreType.DMA
-    pairs = [(9,), (4, 4), (X,), (6,), (5,)]
+    pairs = [(7,), (4, 4), (X,), (X,), (5,)]
     return pl.pallas_call(
         krylov_kernel,
         out_shape=(
@@ -467,8 +428,7 @@
             pltpu.VMEM((8, 256, 256), F32),
             pltpu.VMEM((X, 256, 256), F32),
             pltpu.VMEM((X, 256, 256), BF16),
-            pltpu.VMEM((2, HALF, 256), BF16),
-            pltpu.VMEM((2, 256, 256), BF16),
+            pltpu.VMEM((X, 256, 256), BF16),
             pltpu.VMEM((8, 4, 16, 128), BF16),
             pltpu.VMEM((8, 4, 16, 128), BF16),
             pltpu.VMEM((8,) + cell, F32),

time: 98.2 us -> 98.2 us (level)
  no operation moved by 1% of the time
where the time goes in v7:
time: 98.2 us; the launch traced here: 98 us
  Pallas kernels  96.7 us (98%)
  between operations  1.34 us (1%)
    pallas_call x1, Pallas kernels, krylov(): pl.pallas_call(krylov_kernel, out_shape=(jax.ShapeDtypeStruct((256, 256),...  82.3 us
    pallas_call x1, Pallas kernels, factor_call(): pl.pallas_call(factor_kernel, out_shape=(jax.ShapeDtypeStruct((256, 256),...  8.6 us
    pallas_call x1, Pallas kernels, dense_tile(): pl.pallas_call(dense_kernel, grid=(NB // STEP,), out_shape=jax.ShapeDtype...  5.76 us

profile of v7, /device:TPU:1, one launch (start us, length us, event | category | flops | bytes accessed | tf_op | source)
XLA Modules:
  0.0 98.0 jit_solution(3150536802937952452)
XLA Ops:
  0.6 0.0 copy-start
  1.3 5.8 %dense_tile.1.dense_ref = bf16[8,1024,256]{2,1,0:T(8,128)(2,1)} custom-call(s32[96]{0:T(128)} %bitcast.6, s32[96]{0:T(128)} %bitcast.7, s32[1]{0:T(128)} %bitcast.4.count_ref, bf16[96,128,128]{2,1,0:T(8,128)(2,1)} %bitcast.5), custom_call_target="tpu_custom_call" | custom-call | tf_op jit(solution)/shard_map/dense_tile/pallas_call | solution.py:108
  7.1 0.0 copy-done
  7.1 82.3 %krylov.1 = (f32[256,256]{1,0:T(8,128)S(1)}, f32[8,8,8,128]{3,2,1,0:T(8,128)S(1)}) custom-call(bf16[256,256]{1,0:T(8,128)(2,1)S(1)} %copy-done, bf16[8,1024,256]{2,1,0:T(8,128)(2,1)} %dense_tile.1.dense_ref), custom_call_target="tpu_custom_call" | custom-call | tf_op jit(solution)/shard_map/krylov/pallas_call | solution.py:407
  89.4 8.6 %factor.1 = (f32[256,256]{1,0:T(8,128)}, f32[256,256]{1,0:T(8,128)}) custom-call(f32[8,8,8,128]{3,2,1,0:T(8,128)S(1)} %get-tuple-element.4.gram_ref, f32[256,256]{1,0:T(8,128)S(1)} %get-tuple-element.5.items_ref), custom_call_target="tpu_custom_call" | custom-call | tf_op jit(solution)/shard_map/factor/pallas_call | solution.py:537
Async XLA Ops:
  0.6 6.5 %copy-start = (bf16[256,256]{1,0:T(8,128)(2,1)S(1)}, bf16[256,256]{1,0:T(8,128)(2,1)}, u32[]{:S(2)}) copy-start(bf16[256,256]{1,0:T(8,128)(2,1)} %own_ref.1) | copy-start | bytes 393220

commit v8 on v7

--- a/solution.py
+++ b/solution.py
@@ -15,6 +15,7 @@
 GROUP = 8
 STEP = 24
 X, Y, Z = 4, 8, 8
+HALF = 128
 
 
 def vmem():
@@ -67,7 +68,7 @@
     def _():
         acc_ref[...] = jnp.zeros_like(acc_ref)
 
-    count = count_ref[0]
+    count = count_ref[0, 0]
 
     def group(g, carry):
         for j in range(GROUP):
@@ -135,7 +136,7 @@
 def krylov_kernel(
     own_ref, dense_ref, items_ref, gram_ref,
     tile, panel, turned, acc, part, got1, sum1, got2, mine, wide, whole, users,
-    value, near, pack, far, cut, gram1, gsum1, gram2, gsum2, gram3, gsum3, gwide,
+    value, near, pack, relay, far, cut, gram1, gsum1, gram2, gsum2, gram3, gsum3, gwide,
     load, send_p, recv_p, send_u, recv_u, send_a, recv_a, send_b, recv_b, send_g, recv_g,
 ):
     row, col, y, z = places()
@@ -144,6 +145,8 @@
     partner = (chip * 2 + other, col)
     spots = {"r": row, "y": y, "z": z}
 
+    low, high = pl.ds(0, HALF), pl.ds(HALF, HALF)
+
     def spot(i, which):
         return ring(chip, i, X) * 2 + which
 
@@ -184,20 +187,26 @@
 
         lax.fori_loop(0, 7, step, 0)
 
+    prev, nxt, over = spot(3, core), spot(1, core), spot(2, core)
+    last = spot(2, other)
     p = (send_p, recv_p)
-    hops = [(turned, panel.at[row], partner)]
-    hops += [(turned, panel.at[row], beside(i)) for i in (1, 2, 3)]
-    hops += [(panel.at[spot(X - i, core)], panel.at[spot(X - i, core)], partner) for i in (1, 2, 3)]
-
-    def came(n):
-        chips, which = (0, other) if n == 0 else (X - n, core) if n < X else (2 * X - 1 - n, other)
-        landed(panel.at[spot(chips, which)], *p, n)
+    hops = [
+        (turned, panel.at[row], partner),
+        (turned, panel.at[row], beside(1)),
+        (turned, panel.at[row], beside(3)),
+        (panel.at[prev, low], panel.at[prev, low], beside(1)),
+        (panel.at[nxt, high], panel.at[nxt, high], beside(3)),
+        (panel.at[prev], panel.at[prev], partner),
+        (panel.at[nxt], panel.at[nxt], partner),
+        (panel.at[over, low], panel.at[over, low], partner),
+        (panel.at[over, high], panel.at[over, high], partner),
+    ]
 
     def hop(n):
         src, dst, device = hops[n]
         return remote(src, dst, send_p.at[n], recv_p.at[n], device)
 
-    for n in (2, 1, 3, 0):
+    for n in (1, 2, 0):
         hop(n).start()
     panel[row] = turned[...]
     acc[...] = jnp.zeros_like(acc)
@@ -208,31 +217,36 @@
 
         @pl.when(n == 1)
         def _():
-            came(0)
+            landed(panel.at[spot(0, other)], *p, 0)
 
         @pl.when(n == 2)
         def _():
-            came(1)
+            landed(panel.at[prev], *p, 1)
+            hop(3).start()
+            landed(panel.at[nxt], *p, 2)
             hop(4).start()
-            came(3)
+            hop(5).start()
             hop(6).start()
 
         @pl.when(n == 3)
         def _():
-            came(4)
+            landed(panel.at[spot(3, other)], *p, 5)
 
         @pl.when(n == 4)
         def _():
-            came(2)
-            hop(5).start()
+            landed(panel.at[over, low], *p, 3)
+            hop(7).start()
+            landed(panel.at[over, high], *p, 4)
+            hop(8).start()
 
         @pl.when(n == 5)
         def _():
-            came(6)
+            landed(panel.at[spot(1, other)], *p, 6)
 
         @pl.when(n == 7)
         def _():
-            came(5)
+            landed(panel.at[last, low], *p, 7)
+            landed(panel.at[last, high], *p, 8)
 
         q = place(digit)
         acc[...] += lax.dot_general(
@@ -287,7 +301,7 @@
         users_start(0, pair)
     for h in range(4):
         got1[h, me[h]] = part[h, me[h]]
-    for n in range(7):
+    for n in range(9):
         hop(n).wait_send()
     for pair in pairs:
         for h in pair:
@@ -316,11 +330,23 @@
     for h in range(4):
         users_all(3, h).wait_recv()
 
+    b = (send_b, recv_b)
+
     def lend(i):
         return remote(value.at[2 * i + 1], near.at[i], send_a.at[i], recv_a.at[i], partner)
 
-    def pass_on(i):
-        return remote(pack.at[i], far.at[i], send_b.at[i], recv_b.at[i], beside(i))
+    moves = [
+        (pack.at[2, low], relay.at[0], beside(1)),
+        (pack.at[2, high], relay.at[1], beside(3)),
+        (pack.at[1, high], far.at[0, high], beside(1)),
+        (pack.at[3, low], far.at[1, low], beside(3)),
+        (pack.at[1, low], far.at[0, low], beside(1)),
+        (pack.at[3, high], far.at[1, high], beside(3)),
+    ]
+
+    def pass_on(n):
+        src, dst, device = moves[n]
+        return remote(src, dst, send_b.at[n], recv_b.at[n], device)
 
     def meet(i):
         landed(near.at[i], send_a, recv_a, i)
@@ -337,24 +363,44 @@
             def _(i=i):
                 lend(i).start()
 
-        for step, i in ((3, 2), (5, 1), (6, 3)):
-            @pl.when(n == step)
-            def _(i=i):
-                meet(i)
-                pack[i] = near[i].astype(BF16)
-                pass_on(i).start()
+        @pl.when(n == 3)
+        def _():
+            meet(2)
+            pack[2] = near[2].astype(BF16)
+            pass_on(0).start()
+            pass_on(1).start()
+
+        @pl.when(n == 5)
+        def _():
+            meet(1)
+            pack[1, HALF:] = near[1, HALF:].astype(BF16)
+            pass_on(2).start()
+
+        @pl.when(n == 6)
+        def _():
+            meet(3)
+            pack[3, :HALF] = near[3, :HALF].astype(BF16)
+            pass_on(3).start()
 
         return lax.div(digits, 8)
 
     lax.fori_loop(0, 8, transposed, table(BACKWARD))
+    landed(relay.at[0], *b, 0)
+    pack[1, :HALF] = (near[1, :HALF] + relay[0].astype(F32)).astype(BF16)
+    pass_on(4).start()
+    landed(relay.at[1], *b, 1)
+    pack[3, HALF:] = (near[3, HALF:] + relay[1].astype(F32)).astype(BF16)
+    pass_on(5).start()
     meet(0)
+
     users_left(3)
     for i in range(X):
         lend(i).wait_send()
-    items = near[0]
-    for i in (1, 3, 2):
-        landed(far.at[i], send_b, recv_b, i)
-        items = items + far[i].astype(F32)
+    landed(far.at[0, high], *b, 2)
+    landed(far.at[1, low], *b, 3)
+    landed(far.at[0, low], *b, 4)
+    landed(far.at[1, high], *b, 5)
+    items = near[0] + far[0].astype(F32) + far[1].astype(F32)
     items_ref[...] = items
 
     gram = lax.dot_general(
@@ -384,8 +430,8 @@
         if n:
             spread_all(n - 1).wait_send()
         else:
-            for i in (1, 2, 3):
-                pass_on(i).wait_send()
+            for k in range(6):
+                pass_on(k).wait_send()
         spread_all(n).wait_recv()
 
     move(0)
@@ -403,7 +449,7 @@
 def krylov(own, tile):
     cell = (8, 128)
     dma = pltpu.SemaphoreType.DMA
-    pairs = [(7,), (4, 4), (X,), (X,), (5,)]
+    pairs = [(9,), (4, 4), (X,), (6,), (5,)]
     return pl.pallas_call(
         krylov_kernel,
         out_shape=(
@@ -428,7 +474,8 @@
             pltpu.VMEM((8, 256, 256), F32),
             pltpu.VMEM((X, 256, 256), F32),
             pltpu.VMEM((X, 256, 256), BF16),
-            pltpu.VMEM((X, 256, 256), BF16),
+            pltpu.VMEM((2, HALF, 256), BF16),
+            pltpu.VMEM((2, 256, 256), BF16),
             pltpu.VMEM((8, 4, 16, 128), BF16),
             pltpu.VMEM((8, 4, 16, 128), BF16),
             pltpu.VMEM((8,) + cell, F32),
@@ -449,6 +496,12 @@
 
 PANEL = 32
 N = 256
+
+
+def inverted(x):
+    guess = pl.reciprocal(x, approx=True)
+    guess = guess * (2.0 - x * guess)
+    return guess * (2.0 - x * guess)
 
 
 def factor_kernel(gram_ref, items_ref, basis_ref, factor_ref, a_ref, d_ref):
@@ -477,8 +530,8 @@
                 one, two = columns[a], columns[a + 1]
                 p11, p12 = one[a : a + 1, :], two[a : a + 1, :]
                 p21, p22 = one[a + 1 : a + 2, :], two[a + 1 : a + 2, :]
-                inv1 = 1.0 / p11
-                inv2 = p11 * (1.0 / (p11 * p22 - p21 * p12))
+                inv1 = inverted(p11)
+                inv2 = p11 * inverted(p11 * p22 - p21 * p12)
                 ratio = p21 * inv1
                 m1 = jnp.where(sub1 > r, one * inv1, 0.0)
                 m2 = jnp.where(sub1 > r + 1, (two - m1 * p12) * inv2, 0.0)
@@ -549,7 +602,7 @@
 
 
 def local(blocks, block_row, block_col, counts, start_block):
-    tile = dense_tile(block_row[0, 0], block_col[0, 0], counts[0], blocks[0, 0])
+    tile = dense_tile(block_row[0, 0], block_col[0, 0], counts, blocks[0, 0])
     items, gram = krylov(start_block, tile)
     return factor_call(gram, items)
 

time: 98.2 us -> 98.3 us (level)
  no operation moved by 1% of the time
where the time goes in v8:
time: 98.3 us; the launch traced here: 98.2 us
  Pallas kernels  96.8 us (98%)
  between operations  1.34 us (1%)
    pallas_call x1, Pallas kernels, krylov(): pl.pallas_call(krylov_kernel, out_shape=(jax.ShapeDtypeStruct((256, 256),...  81.8 us
    pallas_call x1, Pallas kernels, factor_call(): pl.pallas_call(factor_kernel, out_shape=(jax.ShapeDtypeStruct((256, 256),...  9.21 us
    pallas_call x1, Pallas kernels, dense_tile(): pl.pallas_call(dense_kernel, grid=(NB // STEP,), out_shape=jax.ShapeDtype...  5.76 us

profile of v8, /device:TPU:1, one launch (start us, length us, event | category | flops | bytes accessed | tf_op | source)
XLA Modules:
  0.0 98.2 jit_solution(7586976087958263658)
XLA Ops:
  0.6 0.0 copy-start
  1.3 5.8 %dense_tile.1.dense_ref = bf16[8,1024,256]{2,1,0:T(8,128)(2,1)} custom-call(s32[96]{0:T(128)} %bitcast.4, s32[96]{0:T(128)} %bitcast.5, s32[1,1]{1,0:T(1,128)S(6)} %copy.7.count_ref, bf16[96,128,128]{2,1,0:T(8,128)(2,1)} %bitcast.3), custom_call_target="tpu_custom_call" | custom-call | tf_op jit(solution)/shard_map/dense_tile/pallas_call | solution.py:109
  7.1 0.0 copy-done
  7.1 81.8 %krylov.1 = (f32[256,256]{1,0:T(8,128)S(1)}, f32[8,8,8,128]{3,2,1,0:T(8,128)S(1)}) custom-call(bf16[256,256]{1,0:T(8,128)(2,1)S(1)} %copy-done, bf16[8,1024,256]{2,1,0:T(8,128)(2,1)} %dense_tile.1.dense_ref), custom_call_target="tpu_custom_call" | custom-call | tf_op jit(solution)/shard_map/krylov/pallas_call | solution.py:453
  89.0 9.2 %factor.1 = (f32[256,256]{1,0:T(8,128)}, f32[256,256]{1,0:T(8,128)}) custom-call(f32[8,8,8,128]{3,2,1,0:T(8,128)S(1)} %get-tuple-element.4.gram_ref, f32[256,256]{1,0:T(8,128)S(1)} %get-tuple-element.5.items_ref), custom_call_target="tpu_custom_call" | custom-call | tf_op jit(solution)/shard_map/factor/pallas_call | solution.py:590
Async XLA Ops:
  0.6 6.5 %copy-start = (bf16[256,256]{1,0:T(8,128)(2,1)S(1)}, bf16[256,256]{1,0:T(8,128)(2,1)}, u32[]{:S(2)}) copy-start(bf16[256,256]{1,0:T(8,128)(2,1)} %own_ref.1) | copy-start | bytes 393220

commit v9 on v8

--- a/solution.py
+++ b/solution.py
@@ -498,12 +498,6 @@
 N = 256
 
 
-def inverted(x):
-    guess = pl.reciprocal(x, approx=True)
-    guess = guess * (2.0 - x * guess)
-    return guess * (2.0 - x * guess)
-
-
 def factor_kernel(gram_ref, items_ref, basis_ref, factor_ref, a_ref, d_ref):
     for k in range(32):
         for c in range(2):
@@ -530,8 +524,8 @@
                 one, two = columns[a], columns[a + 1]
                 p11, p12 = one[a : a + 1, :], two[a : a + 1, :]
                 p21, p22 = one[a + 1 : a + 2, :], two[a + 1 : a + 2, :]
-                inv1 = inverted(p11)
-                inv2 = p11 * inverted(p11 * p22 - p21 * p12)
+                inv1 = 1.0 / p11
+                inv2 = p11 * (1.0 / (p11 * p22 - p21 * p12))
                 ratio = p21 * inv1
                 m1 = jnp.where(sub1 > r, one * inv1, 0.0)
                 m2 = jnp.where(sub1 > r + 1, (two - m1 * p12) * inv2, 0.0)

time: 98.3 us -> 97.7 us (level)
  no operation moved by 1% of the time
where the time goes in v9:
time: 97.7 us; the launch traced here: 97.6 us
  Pallas kernels  96.2 us (98%)
  between operations  1.34 us (1%)
    pallas_call x1, Pallas kernels, krylov(): pl.pallas_call(krylov_kernel, out_shape=(jax.ShapeDtypeStruct((256, 256),...  81.8 us
    pallas_call x1, Pallas kernels, factor_call(): pl.pallas_call(factor_kernel, out_shape=(jax.ShapeDtypeStruct((256, 256),...  8.6 us
    pallas_call x1, Pallas kernels, dense_tile(): pl.pallas_call(dense_kernel, grid=(NB // STEP,), out_shape=jax.ShapeDtype...  5.76 us

profile of v9, /device:TPU:1, one launch (start us, length us, event | category | flops | bytes accessed | tf_op | source)
XLA Modules:
  0.0 97.6 jit_solution(12372083394899502084)
XLA Ops:
  0.6 0.0 copy-start
  1.3 5.8 %dense_tile.1.dense_ref = bf16[8,1024,256]{2,1,0:T(8,128)(2,1)} custom-call(s32[96]{0:T(128)} %bitcast.4, s32[96]{0:T(128)} %bitcast.5, s32[1,1]{1,0:T(1,128)S(6)} %copy.7.count_ref, bf16[96,128,128]{2,1,0:T(8,128)(2,1)} %bitcast.3), custom_call_target="tpu_custom_call" | custom-call | tf_op jit(solution)/shard_map/dense_tile/pallas_call | solution.py:109
  7.1 0.0 copy-done
  7.1 81.8 %krylov.1 = (f32[256,256]{1,0:T(8,128)S(1)}, f32[8,8,8,128]{3,2,1,0:T(8,128)S(1)}) custom-call(bf16[256,256]{1,0:T(8,128)(2,1)S(1)} %copy-done, bf16[8,1024,256]{2,1,0:T(8,128)(2,1)} %dense_tile.1.dense_ref), custom_call_target="tpu_custom_call" | custom-call | tf_op jit(solution)/shard_map/krylov/pallas_call | solution.py:453
  89.0 8.6 %factor.1 = (f32[256,256]{1,0:T(8,128)}, f32[256,256]{1,0:T(8,128)}) custom-call(f32[8,8,8,128]{3,2,1,0:T(8,128)S(1)} %get-tuple-element.4.gram_ref, f32[256,256]{1,0:T(8,128)S(1)} %get-tuple-element.5.items_ref), custom_call_target="tpu_custom_call" | custom-call | tf_op jit(solution)/shard_map/factor/pallas_call | solution.py:584
Async XLA Ops:
  0.6 6.5 %copy-start = (bf16[256,256]{1,0:T(8,128)(2,1)S(1)}, bf16[256,256]{1,0:T(8,128)(2,1)}, u32[]{:S(2)}) copy-start(bf16[256,256]{1,0:T(8,128)(2,1)} %own_ref.1) | copy-start | bytes 393220
